TPU v7x, 128 devices: a whole 4x4x4 slice. The times are simulated.
128 devices in a mesh: de: 32 (over x, z, core), tp: 4 (over y).
Axes of the slice: x: 4, y: 4, z: 4, core: 2. Of those that a mesh axis runs over, the one named last changes fastest.
Arguments:
- raw_tiles: bfloat16 [4, 512, 512], P(None, ('de', 'tp')), may hold values from -6 to 6
- stem_weight: bfloat16 [48, 4, 3, 3], replicated, may hold values from -1 to 1
- embed_weight: bfloat16 [768, 1024], replicated, may hold values from -0.21875 to 0.21875
- norm_gain: float32 [1024], replicated, may hold values from 0.1 to 1.9
- router_weight: bfloat16 [1024, 32], replicated, may hold values from -0.1875 to 0.1875
- w_gate: bfloat16 [32, 1024, 4096], P('de', None, 'tp'), may hold values from -0.1875 to 0.1875
- w_up: bfloat16 [32, 1024, 4096], P('de', None, 'tp'), may hold values from -0.1875 to 0.1875
- w_down: bfloat16 [32, 4096, 1024], P('de', 'tp'), may hold values from -0.09375 to 0.09375
- routes: int32 [16384, 1], P(('de', 'tp')), may hold values from 0 to 31; in each aligned block of 128 rows (0 to 127, 128 to 255, ...) at most 8 rows name the same one
- cotangent: bfloat16 [16384, 1024], P(('de', 'tp')), may hold values from -6 to 6
Outputs:
- expert_mix: bfloat16 [16384, 1024], P(('de', 'tp'))
- grad_gate: float32 [32, 1024, 4096], P('de', None, 'tp')
- grad_up: float32 [32, 1024, 4096], P('de', None, 'tp')
- grad_down: float32 [32, 4096, 1024], P('de', 'tp')
- grad_router: float32 [1024, 32], replicated
- grad_gain: float32 [1024], replicated
- grad_embed: float32 [768, 1024], replicated
- grad_stem: float32 [48, 4, 3, 3], replicated
Inputs may be any that keep to these rules, and one draw needn't show every extreme that they name: `routes`: within the tokens of one tile no expert is named more than 8 times, and in every draw some expert is named exactly 8 times in some tile.
All inputs are finite; a program needn't handle non-finite values.
Results may differ from a plain program's by a relative error of at most 0.0092.
Values may be sent and summed in bfloat16 or wider, within the bound.
No kernel may reach another device: no remote copies, remote signals or barrier semaphores. Data moves between devices by JAX's collectives and lax.ppermute only.
A program may use at most 128 MiB of HBM per device.

v0:
```python
import jax
import jax.numpy as jnp
from jax import lax
from jax.sharding import PartitionSpec as P

PATCH = 4


GELU_C = 0.7978845608028654
GELU_A = 0.044715
EPSILON = 1e-06


def padded_2(block, sides, width):
    for axis, dim in sides:
        count = lax.axis_size(axis)
        forward = [(i, i + 1) for i in range(count - 1)]
        backward = [(target, source) for source, target in forward]
        low = lax.ppermute(
            lax.slice_in_dim(block, block.shape[dim] - width, None, axis=dim), axis, forward
        )
        high = lax.ppermute(lax.slice_in_dim(block, 0, width, axis=dim), axis, backward)
        block = jnp.concatenate([low, block, high], axis=dim)
    return block


def gelu_value(preact):
    tanh_v = jnp.tanh(GELU_C * (preact + GELU_A * preact * preact * preact))
    return 0.5 * preact * (1.0 + tanh_v)


def gelu_slope(preact):
    tanh_v = jnp.tanh(GELU_C * (preact + GELU_A * preact * preact * preact))
    return 0.5 * (1.0 + tanh_v) + 0.5 * preact * (1.0 - tanh_v * tanh_v) * GELU_C * (
        1.0 + 3.0 * GELU_A * preact * preact
    )


def stem_stack(padded):
    pixel_rows = padded.shape[1] - 2
    pixel_cols = padded.shape[2]
    widened = jnp.pad(padded, ((0, 0), (0, 0), (1, 1)))
    pieces = [
        widened[:, row_step : row_step + pixel_rows, col_step : col_step + pixel_cols]
        for row_step in range(3)
        for col_step in range(3)
    ]
    stacked = jnp.stack(pieces, axis=1)
    return stacked.reshape(36, pixel_rows * pixel_cols)


def patchify(feature_b, pixel_rows, pixel_cols):
    channels = feature_b.shape[0]
    patch_grid = feature_b.reshape(channels, pixel_rows // PATCH, PATCH, pixel_cols // PATCH, PATCH)
    patch_grid = patch_grid.transpose(1, 3, 0, 2, 4)
    return patch_grid.reshape(pixel_rows // PATCH * (pixel_cols // PATCH), channels * PATCH * PATCH)


def unpatchify(patch_cot, pixel_rows, pixel_cols, channels):
    patch_grid = patch_cot.reshape(pixel_rows // PATCH, pixel_cols // PATCH, channels, PATCH, PATCH)
    patch_grid = patch_grid.transpose(2, 0, 3, 1, 4)
    return patch_grid.reshape(channels, pixel_rows * pixel_cols)


def front(padded, stem_weight, embed_weight, norm_gain):
    pixel_rows = padded.shape[1] - 2
    pixel_cols = padded.shape[2]
    stacked = stem_stack(padded)
    kernel = stem_weight.reshape(stem_weight.shape[0], 36)
    preact = jnp.dot(kernel, stacked, preferred_element_type=jnp.float32)
    feature_b = gelu_value(preact).astype(jnp.bfloat16)
    patches_b = patchify(feature_b, pixel_rows, pixel_cols)
    embedded = jnp.dot(patches_b, embed_weight, preferred_element_type=jnp.float32)
    inv_rms = lax.rsqrt(jnp.mean(embedded * embedded, axis=-1, keepdims=True) + EPSILON)
    hidden_b = (embedded * inv_rms * norm_gain).astype(jnp.bfloat16)
    return (stacked, preact, patches_b, embedded, inv_rms, hidden_b)


def back_front(
    stacked,
    preact,
    patches_b,
    embedded,
    inv_rms,
    norm_gain,
    embed_weight,
    upstream,
    pixel_rows,
    pixel_cols,
):
    normed = embedded * inv_rms
    scaled = upstream * norm_gain
    embed_in = inv_rms * (scaled - normed * jnp.mean(scaled * normed, axis=-1, keepdims=True))
    gain_part = jnp.sum(upstream * normed, axis=0)
    embed_cot = embed_in.astype(jnp.bfloat16)
    embed_part = jnp.dot(patches_b.T, embed_cot, preferred_element_type=jnp.float32)
    patch_cot = jnp.dot(embed_cot, embed_weight.T, preferred_element_type=jnp.float32)
    feature_cot = unpatchify(patch_cot, pixel_rows, pixel_cols, preact.shape[0])
    preact_cot = (feature_cot * gelu_slope(preact)).astype(jnp.bfloat16)
    stem_part = jnp.dot(preact_cot, stacked.T, preferred_element_type=jnp.float32)
    return (gain_part, embed_part, stem_part)


def slot_index(route_rows, experts, capacity):
    chosen = route_rows.reshape(-1)
    onehot = (chosen[:, None] == jnp.arange(experts, dtype=jnp.int32)[None, :]).astype(jnp.int32)
    before = jnp.cumsum(onehot, axis=0) - onehot
    slot_pos = jnp.sum(before * onehot, axis=1)
    return chosen * capacity + slot_pos


def gate_scores(logits, routes):
    picked = jnp.take_along_axis(logits, routes, axis=1)
    return jax.nn.sigmoid(picked)


def router_cot(score_grad, gate_score, routes, experts):
    local_grad = score_grad * gate_score * (1.0 - gate_score)
    chosen_hot = (routes[:, :, None] == jnp.arange(experts, dtype=jnp.int32)[None, None, :]).astype(
        jnp.float32
    )
    return jnp.sum(chosen_hot * local_grad[:, :, None], axis=1).astype(jnp.bfloat16)


def dispatch(buffer):
    moved = lax.all_to_all(buffer, "de", split_axis=0, concat_axis=0, tiled=True)
    return lax.all_gather(moved[None], "tp", axis=0, tiled=True)


def collect(partial_term, total_rows, experts, capacity, model_width):
    members = lax.axis_size("tp")
    own_share = lax.psum_scatter(
        partial_term(jnp.int32(0), total_rows // members * lax.axis_size("tp")),
        "tp",
        scatter_dimension=0,
        tiled=True,
    )
    share_b = own_share.astype(jnp.bfloat16).reshape(experts, capacity, model_width)
    returned = lax.all_to_all(share_b, "de", split_axis=0, concat_axis=0, tiled=True)
    return returned.reshape(experts * capacity, model_width)


def local(
    raw_tiles,
    stem_weight,
    embed_weight,
    norm_gain,
    router_weight,
    w_gate,
    w_up,
    w_down,
    routes,
    cotangent,
):
    tok_dev = cotangent.shape[0]
    model_width = cotangent.shape[1]
    top_count = routes.shape[1]
    local_experts = w_gate.shape[0]
    hidden_share = w_gate.shape[2]
    owners = lax.axis_size("de")
    members = lax.axis_size("tp")
    experts = local_experts * owners
    capacity = 2 * tok_dev * top_count // experts
    pixel_rows = raw_tiles.shape[1]
    pixel_cols = raw_tiles.shape[2]
    padded = padded_2(raw_tiles, ((("de", "tp"), 1),), 1)
    stacked, preact, patches_b, embedded, inv_rms, hidden_b = front(
        padded, stem_weight, embed_weight, norm_gain
    )
    logits = jnp.dot(hidden_b, router_weight, preferred_element_type=jnp.float32)
    gate_score = gate_scores(logits, routes)
    slot_flat = slot_index(routes, experts, capacity)
    selector = (
        slot_flat[None, :] == jnp.arange(experts * capacity, dtype=jnp.int32)[:, None]
    ).astype(jnp.bfloat16)
    hidden_pairs = jnp.repeat(hidden_b, top_count, axis=0)
    cot_pairs = jnp.repeat(cotangent.astype(jnp.float32), top_count, axis=0)
    out_cot = (gate_score * cot_pairs).astype(jnp.bfloat16)
    sent_rows = jnp.dot(selector, hidden_pairs, preferred_element_type=jnp.float32).astype(
        jnp.bfloat16
    )
    sent_cots = jnp.dot(selector, out_cot, preferred_element_type=jnp.float32).astype(jnp.bfloat16)
    group_shape = (members, owners, local_experts, capacity, model_width)
    group_rows = dispatch(sent_rows.reshape(experts, capacity, model_width)).reshape(group_shape)
    group_cots = dispatch(sent_cots.reshape(experts, capacity, model_width)).reshape(group_shape)
    gate_proj = jnp.einsum(
        "tslcx,lxf->tslcf", group_rows, w_gate, preferred_element_type=jnp.float32
    )
    up_proj = jnp.einsum("tslcx,lxf->tslcf", group_rows, w_up, preferred_element_type=jnp.float32)
    sigmoid_gate = jax.nn.sigmoid(gate_proj)
    activated = gate_proj * sigmoid_gate
    hidden_act = (activated * up_proj).astype(jnp.bfloat16)
    total_rows = members * owners * local_experts * capacity
    slot_block = local_experts * capacity

    def forward_term(first_row, row_count):
        rows_part = hidden_act.reshape(total_rows, hidden_share)
        rows_part = rows_part.reshape(
            row_count // slot_block, local_experts, capacity, hidden_share
        )
        product = jnp.einsum(
            "blcf,lfx->blcx", rows_part, w_down, preferred_element_type=jnp.float32
        )
        return product.reshape(row_count, model_width)

    out_flat = collect(forward_term, total_rows, experts, capacity, model_width)
    out_wide = jnp.take(out_flat, slot_flat, axis=0).astype(jnp.float32)
    expert_mix = jnp.sum(
        (gate_score * out_wide).reshape(tok_dev, top_count, model_width), axis=1
    ).astype(jnp.bfloat16)
    score_grad = jnp.sum(cot_pairs * out_wide, axis=-1).reshape(tok_dev, top_count)
    logit_cot = router_cot(score_grad, gate_score, routes, experts)
    router_part = jnp.dot(hidden_b.T, logit_cot, preferred_element_type=jnp.float32)
    router_total = lax.psum(router_part, ("de", "tp"))
    act_cot = jnp.einsum("tslcx,lfx->tslcf", group_cots, w_down, preferred_element_type=jnp.float32)
    gate_cot = (
        act_cot * up_proj * (sigmoid_gate * (1.0 + gate_proj * (1.0 - sigmoid_gate)))
    ).astype(jnp.bfloat16)
    up_cot = (act_cot * activated).astype(jnp.bfloat16)
    grad_gate = jnp.einsum(
        "tslcx,tslcf->lxf", group_rows, gate_cot, preferred_element_type=jnp.float32
    )
    grad_up = jnp.einsum("tslcx,tslcf->lxf", group_rows, up_cot, preferred_element_type=jnp.float32)
    grad_down = jnp.einsum(
        "tslcf,tslcx->lfx", hidden_act, group_cots, preferred_element_type=jnp.float32
    )

    def backward_term(first_row, row_count):
        gate_part = gate_cot.reshape(total_rows, hidden_share)
        up_part = up_cot.reshape(total_rows, hidden_share)
        gate_part = gate_part.reshape(
            row_count // slot_block, local_experts, capacity, hidden_share
        )
        up_part = up_part.reshape(row_count // slot_block, local_experts, capacity, hidden_share)
        product = jnp.einsum(
            "blcf,lxf->blcx", gate_part, w_gate, preferred_element_type=jnp.float32
        )
        product = product + jnp.einsum(
            "blcf,lxf->blcx", up_part, w_up, preferred_element_type=jnp.float32
        )
        return product.reshape(row_count, model_width)

    cot_flat = collect(backward_term, total_rows, experts, capacity, model_width)
    cot_back = jnp.take(cot_flat, slot_flat, axis=0).astype(jnp.float32)
    upstream = jnp.sum(cot_back.reshape(tok_dev, top_count, model_width), axis=1)
    upstream = upstream + jnp.dot(logit_cot, router_weight.T, preferred_element_type=jnp.float32)
    gain_part, embed_part, stem_part = back_front(
        stacked,
        preact,
        patches_b,
        embedded,
        inv_rms,
        norm_gain,
        embed_weight,
        upstream,
        pixel_rows,
        pixel_cols,
    )
    gain_total, embed_total, stem_total = lax.psum((gain_part, embed_part, stem_part), ("de", "tp"))
    return (
        expert_mix,
        grad_gate,
        grad_up,
        grad_down,
        router_total,
        gain_total,
        embed_total,
        stem_total.reshape(stem_weight.shape),
    )


def solution(mesh):
    return jax.shard_map(
        local,
        mesh=mesh,
        in_specs=(
            P(None, ("de", "tp"), None),
            P(),
            P(),
            P(),
            P(),
            P("de", None, "tp"),
            P("de", None, "tp"),
            P("de", "tp", None),
            P(("de", "tp"), None),
            P(("de", "tp"), None),
        ),
        out_specs=(
            P(("de", "tp"), None),
            P("de", None, "tp"),
            P("de", None, "tp"),
            P("de", "tp", None),
            P(),
            P(),
            P(),
            P(),
        ),
        check_vma=False,
    )
```

profile of v0, /device:TPU:1, one launch (start us, length us, event | category | flops | bytes accessed | tf_op | source)
XLA Modules:
  0.0 458.3 jit_solution(13598997807210420806)
XLA Ops:
  8.1 4.0 collective-permute-start
  12.2 3.9 collective-permute-start.1
  24.5 2.0 multiply_reduce_fusion.2
  27.6 20.7 %all_to_all.20 = bf16[32,8,1024]{2,1,0:T(8,128)(2,1)} all-to-all(bf16[32,8,1024]{2,1,0:T(8,128)(2,1)S(1)} %fusion.33), channel_id=1, replica_groups=mesh['de'=32,'tp'=4] {'de'}, dimensions={0} | all-to-all | bytes 1048576 | tf_op jit(solution)/shard_map/all_to_all | solution.py:126
  48.6 27.7 %all-gather.5.cloned.1.call-done = bf16[128,8,1024]{2,1,0:T(8,128)(2,1)} async-done(((bf16[32,8,1024]{2,1,0:T(8,128)(2,1)}), bf16[128,8,1024]{2,1,0:T(8,128)(2,1)}) %all-gather.5.cloned.1.call-update) | async-done | bytes 2097168 | tf_op jit(solution)/shard_map/all_gather | solution.py:127
  76.3 4.7 %fusion.13 = f32[4,32,8,1024]{3,2,1,0:T(8,128)S(1)} fusion(bf16[4,32,8,1024]{3,2,1,0:T(8,128)(2,1)} %bitcast.260, bf16[1,1024,1024]{2,1,0:T(8,128)(2,1)} %param.17), kind=kOutput, calls=%fused_computation.30 | convolution fusion | flops 2147483648 | bytes 8388608 | tf_op jit(solution)/shard_map/tslcx,lxf->tslcf/dot_general | solution.py:186
  81.0 4.6 fusion.3
  85.6 3.7 convolution_bitcast_fusion.1
  89.3 4.4 copy.98
  94.5 46.4 %reduce-scatter.3.cloned.1.call-done = f32[256,1024]{1,0:T(8,128)} async-done(((f32[1024,1024]{1,0:T(8,128)}), f32[256,1024]{1,0:T(8,128)}) %reduce-scatter.3.cloned.1.call-update) | async-done | bytes 1048592 | tf_op jit(solution)/shard_map/reduce_scatter | solution.py:132
  140.9 2.1 convert_bitcast_fusion.1
  143.0 7.7 %all-to-all-start.1 = ((bf16[32,8,1024]{2,1,0:T(8,128)(2,1)}), bf16[32,8,1024]{2,1,0:T(8,128)(2,1)S(1)}, u32[]{:S(2)}, u32[]{:S(2)}) async-start(bf16[32,8,1024]{2,1,0:T(8,128)(2,1)} %convert_bitcast_fusion.1), calls=%async_computation.2 | async-start | bytes 1048576 | tf_op jit(solution)/shard_map/all_to_all | solution.py:139
  151.4 1.3 gather_fusion
  152.7 9.6 %all-to-all-done.1 = bf16[32,8,1024]{2,1,0:T(8,128)(2,1)S(1)} async-done(((bf16[32,8,1024]{2,1,0:T(8,128)(2,1)}), bf16[32,8,1024]{2,1,0:T(8,128)(2,1)S(1)}, u32[]{:S(2)}, u32[]{:S(2)}) %all-to-all-start.1) | async-done | bytes 524320 | tf_op jit(solution)/shard_map/all_to_all | solution.py:139
  163.9 15.2 %all_to_all.21 = bf16[32,8,1024]{2,1,0:T(8,128)(2,1)} all-to-all(bf16[32,8,1024]{2,1,0:T(8,128)(2,1)S(1)} %fusion.34), channel_id=1, replica_groups=mesh['de'=32,'tp'=4] {'de'}, dimensions={0} | all-to-all | bytes 1048576 | tf_op jit(solution)/shard_map/all_to_all | solution.py:126
  179.1 26.6 %all-gather.7.cloned.1.call-done = bf16[128,8,1024]{2,1,0:T(8,128)(2,1)} async-done(((bf16[32,8,1024]{2,1,0:T(8,128)(2,1)}), bf16[128,8,1024]{2,1,0:T(8,128)(2,1)}) %all-gather.7.cloned.1.call-update) | async-done | bytes 2097168 | tf_op jit(solution)/shard_map/all_gather | solution.py:127
  205.7 7.1 %fusion.2 = (bf16[4,32,1,8,1024]{4,3,1,0,2:T(8,128)(2,1)S(1)}, bf16[4,32,1,8,1024]{4,3,1,0,2:T(8,128)(2,1)S(1)}) fusion(f32[4,32,8,1024]{3,2,1,0:T(8,128)} %copy-done.32, f32[4,32,8,1024]{3,2,1,0:T(8,128)} %get-tuple-element.44, bf16[4,32,8,1024]{3,2,1,0:T(8,128)(2,1)} %bitcast.264, bf16[1,1024,1024]{2,1,0:T(8,128)(2,1)S(1)} %copy-done), kind=kOutput, calls=%fused_computation.7 | convolution fusion | flops 2161115136 | bytes 16777216 | tf_op jit(solution)/shard_map/tslcx,lfx->tslcf/dot_general | solution.py:215
  212.8 3.8 fusion.15
  216.6 3.8 add_bitcast_fusion
  220.5 4.4 copy.97
  226.8 6.0 %convolution_bitcast_fusion.2 = f32[1,1024,1024]{2,1,0:T(8,128)} fusion(bf16[4,32,8,1024]{3,2,1,0:T(8,128)(2,1)S(1)} %bitcast.265, bf16[4,32,1,8,1024]{4,3,1,0,2:T(8,128)(2,1)} %copy-done.28), kind=kOutput, calls=%fused_computation.23 | convolution fusion | flops 2147483648 | bytes 8388608 | tf_op jit(solution)/shard_map/tslcf,tslcx->lfx/dot_general | solution.py:224
  232.8 39.2 %reduce-scatter.5.cloned.1.call-done = f32[256,1024]{1,0:T(8,128)} async-done(((f32[1024,1024]{1,0:T(8,128)}), f32[256,1024]{1,0:T(8,128)}) %reduce-scatter.5.cloned.1.call-update) | async-done | bytes 1048592 | tf_op jit(solution)/shard_map/reduce_scatter | solution.py:132
  272.0 2.1 convert_bitcast_fusion
  274.1 7.8 %all-to-all-start.3 = ((bf16[32,8,1024]{2,1,0:T(8,128)(2,1)}), bf16[32,8,1024]{2,1,0:T(8,128)(2,1)S(1)}, u32[]{:S(2)}, u32[]{:S(2)}) async-start(bf16[32,8,1024]{2,1,0:T(8,128)(2,1)} %convert_bitcast_fusion), calls=%async_computation.5 | async-start | bytes 1048576 | tf_op jit(solution)/shard_map/all_to_all | solution.py:139
  281.9 6.6 %convolution_bitcast_fusion.3 = f32[1,1024,1024]{2,1,0:T(8,128)} fusion(bf16[4,32,8,1024]{3,2,1,0:T(8,128)(2,1)} %bitcast.261, bf16[4,32,1,8,1024]{4,3,1,0,2:T(8,128)(2,1)} %copy-done.30), kind=kOutput, calls=%fused_computation.24 | convolution fusion | flops 2147483648 | bytes 8388608 | tf_op jit(solution)/shard_map/tslcx,tslcf->lxf/dot_general | solution.py:223
  288.6 4.9 %all-to-all-done.3 = bf16[32,8,1024]{2,1,0:T(8,128)(2,1)S(1)} async-done(((bf16[32,8,1024]{2,1,0:T(8,128)(2,1)}), bf16[32,8,1024]{2,1,0:T(8,128)(2,1)S(1)}, u32[]{:S(2)}, u32[]{:S(2)}) %all-to-all-start.3) | async-done | bytes 524320 | tf_op jit(solution)/shard_map/all_to_all | solution.py:139
  295.3 2.2 fusion.79
  297.6 6.7 %convolution_bitcast_fusion.4 = f32[1,1024,1024]{2,1,0:T(8,128)} fusion(bf16[4,32,8,1024]{3,2,1,0:T(8,128)(2,1)} %bitcast.262, bf16[4,32,1,8,1024]{4,3,1,0,2:T(8,128)(2,1)} %copy-done.29), kind=kOutput, calls=%fused_computation.25 | convolution fusion | flops 2147483648 | bytes 8388608 | tf_op jit(solution)/shard_map/tslcx,tslcf->lxf/dot_general | solution.py:220
  306.1 64.1 %all-reduce.1 = (f32[1024]{0:T(1024)}, f32[48,4,3,3]{0,3,2,1:T(4,128)S(1)}) all-reduce(f32[1024]{0:T(1024)S(1)} %get-tuple-element.26, f32[48,4,3,3]{0,3,2,1:T(4,128)S(1)} %reshape.230), channel_id=1, replica_groups=mesh['de'=32,'tp'=4] {'de','tp'}, use_global_device_ids=true, to_apply=%region_8.10 | all-reduce | flops 2752 | bytes 22016 | tf_op jit(solution)/shard_map/psum | solution.py:259
  370.7 75.2 %all-reduce.5.cloned.1.call-done = (f32[1024,32]{0,1:T(8,128)}, f32[768,1024]{1,0:T(8,128)}) async-done(((f32[1024,32]{0,1:T(8,128)}, f32[768,1024]{1,0:T(8,128)}), (f32[1024,32]{0,1:T(8,128)}, f32[768,1024]{1,0:T(8,128)})) %all-reduce.5.cloned.1.call-update) | async-done | bytes 3276816 | tf_op jit(solution)/shard_map/psum | solution.py:214
  445.9 1.7 copy.109
  447.6 4.0 copy.110
  (127 shorter events, 19.4 us)
Async XLA Ops:
  7.2 78.4 %copy-start = (bf16[1,1024,1024]{2,1,0:T(8,128)(2,1)S(1)}, bf16[1,1024,1024]{2,1,0:T(8,128)(2,1)}, u32[]{:S(2)}) copy-start(bf16[1,1024,1024]{2,1,0:T(8,128)(2,1)} %param.19) | copy-start | bytes 6291460
  7.2 69.1 %all-gather.5.cloned.1.call-start = ((), (), s32[]{:S(2)}) async-start(), calls=%async_computation.8 | async-start | bytes 2621440 | tf_op jit(solution)/shard_map/all_gather | solution.py:127
  8.1 11.1 %collective-permute-start = (bf16[4,1,512]{2,1,0:T(2,128)(2,1)S(1)}, bf16[4,1,512]{2,1,0:T(2,128)(2,1)S(1)}, u32[]{:S(2)}, u32[]{:S(2)}) collective-permute-start(bf16[4,1,512]{2,1,0:T(2,128)(2,1)S(1)} %get-tuple-element.37), channel_id=1, source_target_pairs={{0,1},{1,2},{2,3},{3,4},{4,5},{5,6},{6,7},{7,8},{8,9},{9,10},{10,1... | collective-permute-start | bytes 12296 | tf_op jit(solution)/shard_map/ppermute | solution.py:19
  12.2 7.1 %collective-permute-start.1 = (bf16[4,1,512]{2,1,0:T(2,128)(2,1)S(1)}, bf16[4,1,512]{2,1,0:T(2,128)(2,1)S(1)}, u32[]{:S(2)}, u32[]{:S(2)}) collective-permute-start(bf16[4,1,512]{2,1,0:T(2,128)(2,1)S(1)} %get-tuple-element.38), channel_id=1, source_target_pairs={{1,0},{2,1},{3,2},{4,3},{5,4},{6,5},{7,6},{8,7},{9,8},{10,9},{11,1... | collective-permute-start | bytes 12296 | tf_op jit(solution)/shard_map/ppermute | solution.py:22
  18.5 207.4 %copy-start.17 = (pred[128]{0:T(512)(128)(4,1)}, pred[128]{0:T(512)(128)(4,1)S(1)}, u32[]{:S(2)}) copy-start(pred[128]{0:T(512)(128)(4,1)S(1)} %get-tuple-element.33) | copy-start | bytes 388
  26.5 54.5 %copy-start.21 = (f32[128]{0:T(128)}, f32[128]{0:T(128)S(1)}, u32[]{:S(2)}) copy-start(f32[128]{0:T(128)S(1)} %add_rsqrt_fusion) | copy-start | bytes 1540
  48.3 92.5 %reduce-scatter.3.cloned.1.call-start = ((), (), s32[]{:S(2)}) async-start(), calls=%async_computation.6 | async-start | bytes 5242880 | tf_op jit(solution)/shard_map/reduce_scatter | solution.py:132
  76.3 4.7 %copy-start.23 = (bf16[1,1024,1024]{2,1,0:T(8,128)(2,1)S(1)}, bf16[1,1024,1024]{2,1,0:T(8,128)(2,1)}, u32[]{:S(2)}) copy-start(bf16[1,1024,1024]{2,1,0:T(8,128)(2,1)} %param.18) | copy-start | bytes 6291460
  76.3 4.7 %copy-start.26 = (bf16[128,8,1024]{2,1,0:T(8,128)(2,1)S(1)}, bf16[128,8,1024]{2,1,0:T(8,128)(2,1)}, u32[]{:S(2)}) copy-start(bf16[128,8,1024]{2,1,0:T(8,128)(2,1)} %all-gather.5.cloned.1.call-done) | copy-start | bytes 6291460
  81.0 4.6 %copy-start.32 = (f32[4,32,8,1024]{3,2,1,0:T(8,128)}, f32[4,32,8,1024]{3,2,1,0:T(8,128)S(1)}, u32[]{:S(2)}) copy-start(f32[4,32,8,1024]{3,2,1,0:T(8,128)S(1)} %fusion.13) | copy-start | bytes 12582916
  93.8 57.4 %copy-start.10 = (bf16[1024,32]{0,1:T(8,128)(2,1)S(1)}, bf16[1024,32]{0,1:T(8,128)(2,1)}, u32[]{:S(2)}) copy-start(bf16[1024,32]{0,1:T(8,128)(2,1)} %param.16) | copy-start | bytes 196612
  94.4 68.8 %copy-start.16 = (s32[1024]{0:T(1024)}, s32[1024]{0:T(1024)S(1)}, u32[]{:S(2)}) copy-start(s32[1024]{0:T(1024)S(1)} %pad_clamp_fusion) | copy-start | bytes 12292
  143.0 20.2 %copy-start.7 = (bf16[128,1024]{1,0:T(8,128)(2,1)S(1)}, bf16[128,1024]{1,0:T(8,128)(2,1)}, u32[]{:S(2)}) copy-start(bf16[128,1024]{1,0:T(8,128)(2,1)} %param.21) | copy-start | bytes 786436
  143.0 19.4 %all-to-all-start.1 = ((bf16[32,8,1024]{2,1,0:T(8,128)(2,1)}), bf16[32,8,1024]{2,1,0:T(8,128)(2,1)S(1)}, u32[]{:S(2)}, u32[]{:S(2)}) async-start(bf16[32,8,1024]{2,1,0:T(8,128)(2,1)} %convert_bitcast_fusion.1), calls=%async_computation.2 | async-start | bytes 1048576 | tf_op jit(solution)/shard_map/all_to_all | solution.py:139
  150.7 55.0 %all-gather.7.cloned.1.call-start = ((), (), s32[]{:S(2)}) async-start(), calls=%async_computation.9 | async-start | bytes 2621440 | tf_op jit(solution)/shard_map/all_gather | solution.py:127
  163.5 61.5 %copy-start.19 = (bf16[128]{0:T(256)(128)(2,1)}, bf16[128]{0:T(256)(128)(2,1)S(1)}, u32[]{:S(2)}) copy-start(bf16[128]{0:T(256)(128)(2,1)S(1)} %get-tuple-element.31) | copy-start | bytes 772
  179.0 92.9 %reduce-scatter.5.cloned.1.call-start = ((), (), s32[]{:S(2)}) async-start(), calls=%async_computation.7 | async-start | bytes 5242880 | tf_op jit(solution)/shard_map/reduce_scatter | solution.py:132
  205.7 7.1 %copy-start.24 = (bf16[1,1024,1024]{2,1,0:T(8,128)(2,1)S(1)}, bf16[1,1024,1024]{2,1,0:T(8,128)(2,1)}, u32[]{:S(2)}) copy-start(bf16[1,1024,1024]{2,1,0:T(8,128)(2,1)} %param.18) | copy-start | bytes 6291460
  212.8 3.8 copy-start.30
  212.8 3.8 copy-start.29
  212.8 3.8 copy-start.25
  274.1 19.4 %all-to-all-start.3 = ((bf16[32,8,1024]{2,1,0:T(8,128)(2,1)}), bf16[32,8,1024]{2,1,0:T(8,128)(2,1)S(1)}, u32[]{:S(2)}, u32[]{:S(2)}) async-start(bf16[32,8,1024]{2,1,0:T(8,128)(2,1)} %convert_bitcast_fusion), calls=%async_computation.5 | async-start | bytes 1048576 | tf_op jit(solution)/shard_map/all_to_all | solution.py:139
  281.9 164.0 %all-reduce.5.cloned.1.call-start = ((), (), s32[]{:S(2)}) async-start(), calls=%async_computation.10 | async-start | bytes 6553600 | tf_op jit(solution)/shard_map/psum | solution.py:214
  288.6 6.1 %copy-start.4 = (f32[128,1024]{1,0:T(8,128)S(1)}, f32[128,1024]{1,0:T(8,128)}, u32[]{:S(2)}) copy-start(f32[128,1024]{1,0:T(8,128)} %copy-done.3) | copy-start | bytes 1572868
  288.6 6.1 %copy-start.11 = (bf16[1024,32]{0,1:T(8,128)(2,1)S(1)}, bf16[1024,32]{0,1:T(8,128)(2,1)}, u32[]{:S(2)}) copy-start(bf16[1024,32]{0,1:T(8,128)(2,1)} %param.16) | copy-start | bytes 196612
  288.6 6.1 %copy-start.13 = (f32[1024]{0:T(1024)S(1)}, f32[1024]{0:T(1024)}, u32[]{:S(2)}) copy-start(f32[1024]{0:T(1024)} %param.15) | copy-start | bytes 12292
  288.6 6.1 %copy-start.15 = (s32[128,1]{0,1:T(1,128)S(1)}, s32[128,1]{0,1:T(1,128)}, u32[]{:S(2)}) copy-start(s32[128,1]{0,1:T(1,128)} %param.20) | copy-start | bytes 1540
  288.6 6.1 %copy-start.18 = (pred[128]{0:T(512)(128)(4,1)S(1)}, pred[128]{0:T(512)(128)(4,1)}, u32[]{:S(2)}) copy-start(pred[128]{0:T(512)(128)(4,1)} %copy-done.17) | copy-start | bytes 388
  288.6 6.1 %copy-start.20 = (bf16[128]{0:T(256)(128)(2,1)S(1)}, bf16[128]{0:T(256)(128)(2,1)}, u32[]{:S(2)}) copy-start(bf16[128]{0:T(256)(128)(2,1)} %copy-done.19) | copy-start | bytes 772
  288.6 6.1 %copy-start.22 = (f32[128]{0:T(128)S(1)}, f32[128]{0:T(128)}, u32[]{:S(2)}) copy-start(f32[128]{0:T(128)} %copy-done.21) | copy-start | bytes 1540
  297.5 6.8 %copy-start.2 = (bf16[768,1024]{1,0:T(8,128)(2,1)S(1)}, bf16[768,1024]{1,0:T(8,128)(2,1)}, u32[]{:S(2)}) copy-start(bf16[768,1024]{1,0:T(8,128)(2,1)} %param.14) | copy-start | bytes 4718596
  445.9 5.7 %copy-start.1 = (bf16[1,1024,1024]{2,1,0:T(8,128)(2,1)S(1)}, bf16[1,1024,1024]{2,1,0:T(8,128)(2,1)}, u32[]{:S(2)}) copy-start(bf16[1,1024,1024]{2,1,0:T(8,128)(2,1)} %param.19) | copy-start | bytes 6291460
  (10 other events, 17.9 us)
Sparse Core Ops, SparseCore 0:
  48.5 27.7 all-gather.4
  93.9 46.8 reduce-scatter.2
  179.2 26.4 all-gather.6
  225.1 46.8 reduce-scatter.4
  297.7 148.1 all-reduce.4
where the time goes:
time: 465 us; the launch traced here: 458 us
  waiting for transfers between devices  230 us (49%)
  blocking collectives  99.9 us (21%)
  matrix products  55.4 us (12%)
  starting transfers between devices  24.3 us (5%)
  local copies, waits for them, and re-layouts  24.1 us (5%)
  between operations  14.5 us (3%)
  other arithmetic  10.4 us (2%)
    reduce_scatter x2, waiting for transfers between devices, collect(): lax.psum_scatter(partial_term(jnp.int32(0), total_rows // members * lax.a...  85.6 us
    psum x1, waiting for transfers between devices, local(): router_total = lax.psum(router_part, ('de', 'tp'))  75.2 us
    psum x1, blocking collectives, local(): lax.psum((gain_part, embed_part, stem_part), ('de', 'tp'))  64.1 us
    all_gather x2, waiting for transfers between devices, dispatch(): return lax.all_gather(moved[None], 'tp', axis=0, tiled=True)  54.3 us
    all_to_all x2, blocking collectives, dispatch(): lax.all_to_all(buffer, 'de', split_axis=0, concat_axis=0, tiled=True)  35.8 us
    all_to_all x2, starting transfers between devices, collect(): lax.all_to_all(share_b, 'de', split_axis=0, concat_axis=0, tiled=True)  15.5 us
    all_to_all x2, waiting for transfers between devices, collect(): lax.all_to_all(share_b, 'de', split_axis=0, concat_axis=0, tiled=True)  14.5 us
    unnamed x79, local copies, waits for them, and re-layouts  9.54 us
  transfers between devices with their start and end apart: 9, of which 7 were waited for; matrix products, arithmetic and copies ran while one was open for 6% of the time, Pallas kernels for 0%

commit v1 on v0

v1 whole, which is shorter than its diff:
```python
import jax
import jax.numpy as jnp
import numpy as np
from jax import lax
from jax.sharding import PartitionSpec as P

PATCH = 4
GELU_C = 0.7978845608028654
GELU_A = 0.044715
EPSILON = 1e-06
BF = jnp.bfloat16
F32 = jnp.float32
PIX = 144
DE = ("xz", "core")
ALL = ("tp", "xz", "core")
DE_TP = ("xz", "core", "tp")
HALF = ("xz", "tp")


def dot(a, b, dims=((1,), (0,))):
    return lax.dot_general(a, b, (dims, ((), ())), preferred_element_type=F32)


def halo_rows(raw):
    count = lax.axis_size(DE_TP)
    forward = [(i, i + 1) for i in range(count - 1)]
    backward = [(target, source) for source, target in forward]
    low = lax.ppermute(raw[:, -1:], DE_TP, forward)
    high = lax.ppermute(raw[:, :1], DE_TP, backward)
    return jnp.concatenate([low, raw, high], axis=1)


def window_rows(padded, tokens):
    chans, rows, cols = padded.shape
    flat = padded.reshape(chans * rows, cols)
    step = lax.broadcasted_iota(jnp.int32, (6, tokens, cols), 0)
    token = lax.broadcasted_iota(jnp.int32, (6, tokens, cols), 1)
    col = lax.broadcasted_iota(jnp.int32, (6, tokens, cols), 2)
    pick = (col == PATCH * token + step - 1).astype(BF)
    out = lax.dot_general(pick, flat, (((2,), (1,)), ((), ())), preferred_element_type=F32)
    return out.transpose(1, 0, 2).reshape(tokens, 6 * chans * rows).astype(BF)


def placement():
    place = np.zeros((6, 4, 6, 16, 4, 3, 3), np.float32)
    for r in range(4):
        for c in range(4):
            for a in range(3):
                for b in range(3):
                    for i in range(4):
                        place[c + b, i, r + a, r * 4 + c, i, a, b] = 1
    return place.reshape(PIX, 16 * 36)


def cell_mask(channels):
    cell = lax.broadcasted_iota(jnp.int32, (16, channels * 16), 0)
    col = lax.broadcasted_iota(jnp.int32, (16, channels * 16), 1)
    return cell == col % 16


def spread(channels):
    chan = lax.broadcasted_iota(jnp.int32, (channels, channels * 16), 0)
    col = lax.broadcasted_iota(jnp.int32, (channels, channels * 16), 1)
    return (chan == col // 16).astype(BF)


def stem_matrix(stem_weight):
    channels = stem_weight.shape[0]
    taps = stem_weight.reshape(channels, 36)
    wide = dot(taps, spread(channels), ((0,), (0,))).astype(BF)
    stack = jnp.where(cell_mask(channels)[:, None, :], wide[None], BF(0))
    return dot(jnp.asarray(placement(), BF), stack.reshape(16 * 36, channels * 16)).astype(BF)


def stem_gather(product):
    channels = product.shape[1] // 16
    cells = dot(jnp.asarray(placement(), BF), product.astype(BF), ((0,), (0,)))
    cells = cells.reshape(16, 36, channels * 16)
    wide = jnp.sum(jnp.where(cell_mask(channels)[:, None, :], cells, 0.0), axis=0)
    return dot(spread(channels), wide.astype(BF), ((1,), (1,)))


def slots_of(route, experts, capacity):
    tokens = route.shape[0]
    hot = (route[:, None] == jnp.arange(experts, dtype=jnp.int32)[None, :]).astype(F32)
    row = lax.broadcasted_iota(jnp.int32, (tokens, tokens), 0)
    col = lax.broadcasted_iota(jnp.int32, (tokens, tokens), 1)
    before = dot((col < row).astype(BF), hot.astype(BF))
    return route * capacity + jnp.sum(before * hot, axis=1).astype(jnp.int32)


def swap(block):
    count = lax.axis_size("core")
    return lax.ppermute(block, "core", [(i, count - 1 - i) for i in range(count)])


def total_over_all(pieces):
    count = pieces.shape[0] // 2
    core = lax.axis_index("core")
    own = lax.dynamic_slice_in_dim(pieces, core * count, count, axis=0)
    other = lax.dynamic_slice_in_dim(pieces, (1 - core) * count, count, axis=0)
    chip = (own.astype(F32) + swap(other).astype(F32)).astype(BF)
    parts = lax.all_to_all(chip, HALF, split_axis=0, concat_axis=0, tiled=True)
    total = jnp.sum(parts.astype(F32), axis=0).astype(BF)
    copies = jnp.broadcast_to(total[None], parts.shape)
    mine = lax.all_to_all(copies, HALF, split_axis=0, concat_axis=0, tiled=True)
    theirs = swap(mine)
    first = jnp.where(core == 0, mine, theirs)
    second = jnp.where(core == 0, theirs, mine)
    return jnp.concatenate([first, second], axis=0).astype(F32)


def local(
    raw_tiles,
    stem_weight,
    embed_weight,
    norm_gain,
    router_weight,
    w_gate,
    w_up,
    w_down,
    routes,
    cotangent,
):
    tokens, width = cotangent.shape
    owners = lax.axis_size(DE)
    members = lax.axis_size("tp")
    devices = owners * members
    experts = owners
    capacity = 2 * tokens // experts
    slots = experts * capacity
    total = devices * capacity
    w_gate, w_up, w_down = w_gate[0], w_up[0], w_down[0]

    slot_of = slots_of(routes[:, 0], experts, capacity)
    selector = (slot_of[None, :] == jnp.arange(slots, dtype=jnp.int32)[:, None]).astype(BF)
    sent_cots = dot(selector, cotangent).astype(BF)
    moved = lax.all_to_all(
        sent_cots.reshape(experts, capacity, width), DE, split_axis=0, concat_axis=0, tiled=True
    )
    cots = lax.all_gather(moved, "tp", axis=0, tiled=True).reshape(total, width)

    windows = window_rows(halo_rows(raw_tiles), tokens)
    sent_windows = dot(selector, windows).astype(BF).reshape(1, experts, capacity, PIX)
    sent_windows = jnp.broadcast_to(sent_windows, (members, experts, capacity, PIX))
    cells = lax.all_to_all(
        sent_windows.reshape(devices, capacity, PIX), ALL, split_axis=0, concat_axis=0, tiled=True
    ).reshape(total, PIX)

    conv = stem_matrix(stem_weight)
    preact = dot(cells, conv)
    tanh_v = jnp.tanh(GELU_C * (preact + GELU_A * preact * preact * preact))
    patches = (0.5 * preact * (1.0 + tanh_v)).astype(BF)
    embedded = dot(patches, embed_weight)
    inv_rms = lax.rsqrt(jnp.mean(embedded * embedded, axis=-1, keepdims=True) + EPSILON)
    normed = embedded * inv_rms
    hidden = (normed * norm_gain).astype(BF)
    expert = lax.axis_index(DE)
    router_row = lax.dynamic_slice_in_dim(router_weight, expert, 1, axis=1).reshape(1, width)
    logit = jnp.sum(hidden.astype(F32) * router_row.astype(F32), axis=1, keepdims=True)
    score = jax.nn.sigmoid(logit)

    gate_proj = dot(hidden, w_gate)
    up_proj = dot(hidden, w_up)
    sigmoid_gate = jax.nn.sigmoid(gate_proj)
    activated = gate_proj * sigmoid_gate
    hidden_act = (activated * up_proj).astype(BF)
    out_part = dot(hidden_act, w_down).astype(BF)
    out_share = lax.psum_scatter(out_part, "tp", scatter_dimension=0, tiled=True)
    score_share = lax.dynamic_slice_in_dim(score, lax.axis_index("tp") * slots, slots, axis=0)
    mixed = (out_share.astype(F32) * score_share).astype(BF).reshape(experts, capacity, width)
    returned = lax.all_to_all(mixed, DE, split_axis=0, concat_axis=0, tiled=True)
    expert_mix = dot(selector, returned.reshape(slots, width), ((0,), (0,))).astype(BF)

    act_raw = dot(cots, w_down, ((1,), (1,)))
    score_grad = jnp.sum(hidden_act.astype(F32) * act_raw, axis=1, keepdims=True)
    logit_cot = score_grad * score * (1.0 - score)
    act_cot = score * act_raw
    gate_cot = (
        act_cot * up_proj * (sigmoid_gate * (1.0 + gate_proj * (1.0 - sigmoid_gate)))
    ).astype(BF)
    up_cot = (act_cot * activated).astype(BF)
    slot_cot = dot(gate_cot, w_gate, ((1,), (1,))) + dot(up_cot, w_up, ((1,), (1,)))
    upstream = slot_cot + logit_cot * router_row.astype(F32)
    scaled = upstream * norm_gain
    embed_cot = (
        inv_rms * (scaled - normed * jnp.mean(scaled * normed, axis=-1, keepdims=True))
    ).astype(BF)
    gain_part = jnp.sum(upstream * normed, axis=0)
    router_part = jnp.sum(hidden.astype(F32) * logit_cot, axis=0)
    embed_part = dot(patches, embed_cot, ((0,), (0,)))
    feature_cot = dot(embed_cot, embed_weight, ((1,), (1,)))
    slope = 0.5 * (1.0 + tanh_v) + 0.5 * preact * (1.0 - tanh_v * tanh_v) * GELU_C * (
        1.0 + 3.0 * GELU_A * preact * preact
    )
    preact_cot = (feature_cot * slope).astype(BF)
    stem_part = stem_gather(dot(cells, preact_cot, ((0,), (0,))))

    main = embed_part.astype(BF).reshape(16, 48, 8, 128).transpose(0, 2, 1, 3).reshape(128, 48, 128)
    own_expert = jnp.arange(experts, dtype=jnp.int32)[:, None] == expert
    router_rows = jnp.where(own_expert, router_part[None, :], 0.0)
    small = jnp.concatenate([router_rows.reshape(-1), gain_part, stem_part.reshape(-1)]).astype(BF)
    small = jnp.pad(small, (0, 128 * 1024 - small.shape[0])).reshape(128, 8, 128)
    summed = total_over_all(jnp.concatenate([main, small], axis=1))
    embed_total = summed[:, :48].reshape(16, 8, 48, 128).transpose(0, 2, 1, 3).reshape(768, width)
    flat = summed[:, 48:].reshape(-1)
    router_total = flat[: experts * width].reshape(experts, width).T
    gain_total = flat[experts * width : experts * width + width]
    stem_total = flat[experts * width + width : experts * width + width + stem_weight.size]

    grad_gate = dot(hidden, gate_cot, ((0,), (0,)))
    grad_up = dot(hidden, up_cot, ((0,), (0,)))
    out_cot = (score * cots.astype(F32)).astype(BF)
    grad_down = dot(hidden_act, out_cot, ((0,), (0,)))
    return (
        expert_mix,
        grad_gate[None],
        grad_up[None],
        grad_down[None],
        router_total,
        gain_total,
        embed_total,
        stem_total.reshape(stem_weight.shape),
    )


def solution(mesh):
    owners, members = mesh.devices.shape
    fine = jax.sharding.Mesh(mesh.devices.reshape(owners // 2, 2, members), ("xz", "core", "tp"))
    return jax.shard_map(
        local,
        mesh=fine,
        in_specs=(
            P(None, DE_TP, None),
            P(),
            P(),
            P(),
            P(),
            P(DE, None, "tp"),
            P(DE, None, "tp"),
            P(DE, "tp", None),
            P(DE_TP, None),
            P(DE_TP, None),
        ),
        out_specs=(
            P(DE_TP, None),
            P(DE, None, "tp"),
            P(DE, None, "tp"),
            P(DE, "tp", None),
            P(),
            P(),
            P(),
            P(),
        ),
        check_vma=False,
    )
```

time: 465 us -> 221 us (0.48)
  waiting for transfers between devices: 230 us -> 26.7 us
  blocking collectives: 99.9 us -> 24.2 us
  starting transfers between devices: 24.3 us -> 38.7 us
  matrix products: 55.4 us -> 68.8 us
  other arithmetic: 10.4 us -> 15.3 us
    reduce_scatter x2 -> x1, waiting for transfers between devices: 85.6 us -> 0.01 us  [local(): lax.psum_scatter(out_part, 'tp', scatter_dimension=0, tiled=True)]
    psum x1 -> x0, waiting for transfers between devices: 75.2 us -> none  [local(): router_total = lax.psum(router_part, ('de', 'tp'))]
    psum x1 -> x0, blocking collectives: 64.1 us -> none  [local(): lax.psum((gain_part, embed_part, stem_part), ('de', 'tp'))]
    all_gather x2 -> x1, waiting for transfers between devices: 54.3 us -> 1.28 us  [local(): cots = lax.all_gather(moved, 'tp', axis=0, tiled=True).reshape(total, width)]
    dot_general x19 -> x21, matrix products: 55.4 us -> 68.8 us  [the longest x20 68.3 us: dot(): return lax.dot_general(a, b, (dims, ((), ())), preferred_element_type=F32)]
    all_to_all x2 -> x1, blocking collectives: 35.8 us -> 24.2 us  [total_over_all(): parts = lax.all_to_all(chip, HALF, split_axis=0, concat_axis=0, tiled=True)]
    all_to_all x2 -> x4, starting transfers between devices: 15.5 us -> 25.9 us  [the longest x1 9.15 us: local(): lax.all_to_all(sent_cots.reshape(experts, capacity, width), DE, split_axi...]
    all_to_all x2 -> x4, waiting for transfers between devices: 14.5 us -> 24.7 us  [the longest x1 9.75 us: local(): lax.all_to_all(sent_windows.reshape(devices, capacity, PIX), ALL, split_a...]
  transfers between devices with their start and end apart: 9 -> 10, of which waited for: 7 -> 5; matrix products, arithmetic and copies ran while one was open for 6% -> 31% of each run, Pallas kernels for 0% -> 0%
where the time goes in v1:
time: 221 us; the launch traced here: 217 us
  matrix products  68.8 us (31%)
  starting transfers between devices  38.7 us (18%)
  local copies, waits for them, and re-layouts  28.2 us (13%)
  waiting for transfers between devices  26.7 us (12%)
  blocking collectives  24.2 us (11%)
  other arithmetic  15.3 us (7%)
  between operations  14.8 us (7%)
    dot_general x20, matrix products, dot(): return lax.dot_general(a, b, (dims, ((), ())), preferred_element_type=F32)  68.3 us
    all_to_all x1, blocking collectives, total_over_all(): parts = lax.all_to_all(chip, HALF, split_axis=0, concat_axis=0, tiled=True)  24.2 us
    unnamed x50, local copies, waits for them, and re-layouts  14.5 us
    all_to_all x1, waiting for transfers between devices, local(): lax.all_to_all(sent_windows.reshape(devices, capacity, PIX), ALL, split_a...  9.75 us
    all_to_all x1, starting transfers between devices, local(): lax.all_to_all(sent_cots.reshape(experts, capacity, width), DE, split_axi...  9.15 us
    all_to_all x1, waiting for transfers between devices, local(): lax.all_to_all(sent_cots.reshape(experts, capacity, width), DE, split_axi...  9.06 us
    all_to_all x1, starting transfers between devices, total_over_all(): mine = lax.all_to_all(copies, HALF, split_axis=0, concat_axis=0, tiled=True)  8.09 us
    all_to_all x1, starting transfers between devices, local(): lax.all_to_all(sent_windows.reshape(devices, capacity, PIX), ALL, split_a...  4.66 us
  transfers between devices with their start and end apart: 10, of which 5 were waited for; matrix products, arithmetic and copies ran while one was open for 31% of the time, Pallas kernels for 0%

profile of v1, /device:TPU:1, one launch (start us, length us, event | category | flops | bytes accessed | tf_op | source)
XLA Modules:
  0.0 216.8 jit_solution(15329919085254875437)
XLA Ops:
  8.1 4.0 %collective-permute-start = (bf16[4,1,512]{2,1,0:T(2,128)(2,1)S(1)}, bf16[4,1,512]{2,1,0:T(2,128)(2,1)S(1)}, u32[]{:S(2)}, u32[]{:S(2)}) collective-permute-start(bf16[4,1,512]{2,1,0:T(2,128)(2,1)S(1)} %get-tuple-element.42), channel_id=1, source_target_pairs={{0,1},{1,2},{2,3},{3,4},{4,5},{5,6},{6,7},{7,8},{8,9},{9,10},{10,1... | collective-permute-start | bytes 12296 | tf_op jit(solution)/shard_map/ppermute | solution.py:28
  12.1 3.9 %collective-permute-start.1 = (bf16[4,1,512]{2,1,0:T(2,128)(2,1)S(1)}, bf16[4,1,512]{2,1,0:T(2,128)(2,1)S(1)}, u32[]{:S(2)}, u32[]{:S(2)}) collective-permute-start(bf16[4,1,512]{2,1,0:T(2,128)(2,1)S(1)} %get-tuple-element.43), channel_id=1, source_target_pairs={{1,0},{2,1},{3,2},{4,3},{5,4},{6,5},{7,6},{8,7},{9,8},{10,9},{11,1... | collective-permute-start | bytes 12296 | tf_op jit(solution)/shard_map/ppermute | solution.py:29
  17.6 2.0 fusion.31
  19.7 9.2 %all-to-all-start.2 = ((bf16[32,8,1024]{2,1,0:T(8,128)(2,1)}), bf16[32,8,1024]{2,1,0:T(8,128)(2,1)S(1)}, u32[]{:S(2)}, u32[]{:S(2)}) async-start(bf16[32,8,1024]{2,1,0:T(8,128)(2,1)} %fusion.31), calls=%async_computation.3 | async-start | bytes 1048576 | tf_op jit(solution)/shard_map/all_to_all | solution.py:138
  31.4 9.1 %all-to-all-done.2 = bf16[32,8,1024]{2,1,0:T(8,128)(2,1)S(1)} async-done(((bf16[32,8,1024]{2,1,0:T(8,128)(2,1)}), bf16[32,8,1024]{2,1,0:T(8,128)(2,1)S(1)}, u32[]{:S(2)}, u32[]{:S(2)}) %all-to-all-start.2) | async-done | bytes 524320 | tf_op jit(solution)/shard_map/all_to_all | solution.py:138
  41.3 4.7 %all-to-all-start = ((bf16[128,8,144]{2,1,0:T(8,128)(2,1)}), bf16[128,8,144]{2,1,0:T(8,128)(2,1)}, u32[]{:S(2)}, u32[]{:S(2)}) async-start(bf16[128,8,144]{2,1,0:T(8,128)(2,1)} %bitcast.4), calls=%async_computation | async-start | bytes 1048576 | tf_op jit(solution)/shard_map/all_to_all | solution.py:146
  49.2 9.7 %all-to-all-done = bf16[128,8,144]{2,1,0:T(8,128)(2,1)} async-done(((bf16[128,8,144]{2,1,0:T(8,128)(2,1)}), bf16[128,8,144]{2,1,0:T(8,128)(2,1)}, u32[]{:S(2)}, u32[]{:S(2)}) %all-to-all-start) | async-done | bytes 294944 | tf_op jit(solution)/shard_map/all_to_all | solution.py:146
  59.0 3.9 %fusion.33 = f32[1024,768]{1,0:T(8,128)} fusion(bf16[144,576]{1,0:T(8,128)(2,1)S(1)} %copy-done.12, bf16[576,768]{1,0:T(8,128)(2,1)} %select_n.70, bf16[128,8,144]{2,1,0:T(8,128)(2,1)} %all-to-all-done), kind=kOutput, calls=%fused_computation.62 | convolution fusion | flops 354004992 | bytes 4491264 | tf_op jit(solution)/shard_map/dot_general | solution.py:21
  62.9 4.4 %multiply_reduce_fusion.3 = (f32[1024]{0:T(1024)S(1)}, f32[1024,1024]{0,1:T(8,128)S(1)}) fusion(bf16[768,1024]{1,0:T(8,128)(2,1)} %param.14, f32[1024,768]{1,0:T(8,128)} %fusion.33), kind=kOutput, calls=%fused_computation.18 | convolution fusion | flops 1619786752 | bytes 8916992 | tf_op jit(solution)/shard_map/dot_general | solution.py:21
  70.5 4.4 %fusion.16 = f32[1024,1024]{0,1:T(8,128)} fusion(bf16[1024,1024]{0,1:T(8,128)(2,1)S(1)} %get-tuple-element.37, bf16[1,1024,1024]{2,1,0:T(8,128)(2,1)S(1)} %copy-done.14), kind=kOutput, calls=%fused_computation.39 | convolution fusion | flops 2147483648 | bytes 8388608 | tf_op jit(solution)/shard_map/dot_general | solution.py:21
  74.9 4.4 %fusion.20 = f32[1024,1024]{0,1:T(8,128)} fusion(bf16[1024,1024]{0,1:T(8,128)(2,1)S(1)} %get-tuple-element.37, bf16[1,1024,1024]{2,1,0:T(8,128)(2,1)S(1)} %copy-done.16), kind=kOutput, calls=%fused_computation.43 | convolution fusion | flops 2147483648 | bytes 8388608 | tf_op jit(solution)/shard_map/dot_general | solution.py:21
  80.6 8.4 %multiply_reduce_fusion.2 = (f32[1024]{0:T(1024)S(1)}, bf16[1024,1024]{0,1:T(8,128)(2,1)}, bf16[1024,1024]{0,1:T(8,128)(2,1)S(1)}, bf16[1024,1024]{0,1:T(8,128)(2,1)S(1)}) fusion(f32[1024,1024]{0,1:T(8,128)} %fusion.16, f32[1024,1024]{0,1:T(8,128)} %fusion.20, f32[1024]{0:T(1024)S(1)} %add_divide_fusion.1, bf16[1,1024,1024]{2,1,0:T(8,128)(2,1)S(1)} %copy-done, ...), kind=kOutput, calls=%fused_computation.10 | convolution fusion | flops 2167405568 | bytes 18882560 | tf_op jit(solution)/shard_map/dot_general | solution.py:21
  89.1 2.3 %fusion.14 = f32[1024,1024]{0,1:T(8,128)S(1)} fusion(bf16[1024,1024]{0,1:T(8,128)(2,1)S(1)} %get-tuple-element.39, bf16[1,1024,1024]{2,1,0:T(8,128)(2,1)S(1)} %copy-done.15), kind=kOutput, calls=%fused_computation.37 | convolution fusion | flops 2147483648 | bytes 8388608 | tf_op jit(solution)/shard_map/dot_general | solution.py:21
  94.0 3.2 %multiply_reduce_fusion = (bf16[1024]{0:T(1024)(128)(2,1)S(1)}, f32[1024]{0:T(1024)S(1)}, f32[1024,1024]{0,1:T(8,128)S(1)}) fusion(f32[1024,1024]{0,1:T(8,128)S(1)} %copy-done.3, f32[1024]{0:T(1024)S(1)} %add_rsqrt_fusion, f32[1024]{0:T(1024)S(1)} %copy-done.13, f32[1024]{0:T(1024)S(1)} %bitcast.125, f32[1024]{0:T(1024)S(1)} %subtract_multiply_fusion, ...), kind=kOutput, calls=%fused_computation.6 | convolution fusion | flops 2156918784 | bytes 16799744 | tf_op jit(solution)/shard_map/dot_general | solution.py:21
  99.4 3.4 %fusion.29 = bf16[96,8,8,128]{3,1,2,0:T(8,128)(2,1)} fusion(bf16[1024,1024]{0,1:T(8,128)(2,1)S(1)} %multiply_convert_fusion, f32[1024,768]{1,0:T(8,128)S(1)} %copy-done.8), kind=kOutput, calls=%fused_computation.55 | convolution fusion | flops 1618477056 | bytes 6815744 | tf_op jit(solution)/shard_map/dot_general | solution.py:21
  102.8 6.4 %fusion.32 = bf16[144,768]{1,0:T(8,128)(2,1)S(1)} fusion(f32[1024,768]{1,0:T(8,128)} %fusion.33, bf16[1024,1024]{0,1:T(8,128)(2,1)} %copy-done.11, bf16[768,1024]{1,0:T(8,128)(2,1)} %param.14, bf16[128,8,144]{2,1,0:T(8,128)(2,1)} %all-to-all-done), kind=kOutput, calls=%fused_computation.61 | convolution fusion | flops 1852157952 | bytes 7331840 | tf_op jit(solution)/shard_map/dot_general | solution.py:21
  110.9 2.8 %reshape.213 = f32[16,36,768]{2,1,0:T(8,128)} reshape(f32[576,768]{1,0:T(8,128)} %fusion.78) | data formatting | bytes 3538944 | tf_op jit(solution)/shard_map/reshape | solution.py:78
  115.9 1.8 copy.52
  120.2 3.7 %fusion.23 = bf16[1024,1024]{1,0:T(8,128)(2,1)} fusion(bf16[1024,1024]{0,1:T(8,128)(2,1)S(1)} %copy-done.19, bf16[1,1024,1024]{2,1,0:T(8,128)(2,1)S(1)} %copy-done), kind=kOutput, calls=%fused_computation.47 | convolution fusion | flops 2148532224 | bytes 6291456 | tf_op jit(solution)/shard_map/dot_general | solution.py:21
  125.6 24.2 %all_to_all.25 = bf16[64,56,128]{2,1,0:T(8,128)(2,1)S(1)} all-to-all(bf16[64,56,128]{2,1,0:T(8,128)(2,1)S(1)} %add_convert_fusion), channel_id=1, replica_groups=mesh['xz'=16,'core'=2,'tp'=4] {'xz','tp'}, dimensions={0} | all-to-all | bytes 1835008 | tf_op jit(solution)/shard_map/all_to_all | solution.py:103
  151.1 8.1 %all-to-all-start.4 = ((bf16[64,56,128]{2,1,0:T(8,128)(2,1)}), bf16[64,56,128]{2,1,0:T(8,128)(2,1)S(1)}, u32[]{:S(2)}, u32[]{:S(2)}) async-start(bf16[64,56,128]{2,1,0:T(8,128)(2,1)} %broadcast_in_dim.100), calls=%async_computation.5 | async-start | bytes 1835008 | tf_op jit(solution)/shard_map/all_to_all | solution.py:106
  159.3 4.0 %copy.43 = bf16[1024,1024]{0,1:T(8,128)(2,1)} copy(bf16[1024,1024]{1,0:T(8,128)(2,1)} %bitcast.118) | data formatting | bytes 4194304 | tf_op jit(solution)/shard_map/reshape | solution.py:141
  163.2 6.6 %convolution_bitcast_fusion.1 = f32[1,1024,1024]{2,1,0:T(8,128)} fusion(bf16[1024,1024]{0,1:T(8,128)(2,1)} %copy-done.5, bf16[1024,1024]{0,1:T(8,128)(2,1)} %copy-done.21), kind=kOutput, calls=%fused_computation.31 | convolution fusion | flops 2147483648 | bytes 8388608 | tf_op jit(solution)/shard_map/dot_general | solution.py:21
  169.8 4.3 %all-to-all-done.4 = bf16[64,56,128]{2,1,0:T(8,128)(2,1)S(1)} async-done(((bf16[64,56,128]{2,1,0:T(8,128)(2,1)}), bf16[64,56,128]{2,1,0:T(8,128)(2,1)S(1)}, u32[]{:S(2)}, u32[]{:S(2)}) %all-to-all-start.4) | async-done | bytes 917536 | tf_op jit(solution)/shard_map/all_to_all | solution.py:106
  174.1 3.4 %collective-permute-start.3 = (bf16[64,56,128]{2,1,0:T(8,128)(2,1)S(1)}, bf16[64,56,128]{2,1,0:T(8,128)(2,1)S(1)}, u32[]{:S(2)}, u32[]{:S(2)}) collective-permute-start(bf16[64,56,128]{2,1,0:T(8,128)(2,1)S(1)} %all-to-all-done.4), channel_id=1, source_target_pairs={{0,4},{4,0},{1,5},{5,1},{2,6},{6,2},{3,7},{7,3},{8,12},{12,8},{9,1... | collective-permute-start | bytes 2752520 | tf_op jit(solution)/shard_map/ppermute | solution.py:94
  177.6 6.6 %convolution_bitcast_fusion.2 = f32[1,1024,1024]{2,1,0:T(8,128)} fusion(bf16[1024,1024]{0,1:T(8,128)(2,1)} %copy-done.5, bf16[1024,1024]{0,1:T(8,128)(2,1)} %copy-done.18), kind=kOutput, calls=%fused_computation.32 | convolution fusion | flops 2147483648 | bytes 8388608 | tf_op jit(solution)/shard_map/dot_general | solution.py:21
  184.2 4.4 %convolution_bitcast_fusion = f32[1,1024,1024]{2,1,0:T(8,128)} fusion(bf16[1024,1024]{0,1:T(8,128)(2,1)S(1)} %copy-done.20, bf16[1024,1024]{0,1:T(8,128)(2,1)S(1)} %copy-done.9, f32[1024]{0:T(1024)S(1)} %add_divide_fusion.1), kind=kOutput, calls=%fused_computation.30 | convolution fusion | flops 2150629376 | bytes 8392704 | tf_op jit(solution)/shard_map/dot_general | solution.py:21
  188.6 2.4 %broadcast_select_fusion.2 = (bf16[64,56,128]{2,1,0:T(8,128)(2,1)S(1)}, bf16[64,56,128]{2,1,0:T(8,128)(2,1)}) fusion(bf16[64,56,128]{2,1,0:T(8,128)(2,1)} %copy-done.7, bf16[64,56,128]{2,1,0:T(8,128)(2,1)S(1)} %collective-permute-done.3, pred[]{:T(512)S(6)} %eq.72), kind=kLoop, calls=%fused_computation.75 | loop fusion | flops 917504 | bytes 3670017 | tf_op jit(solution)/shard_map/jit(_where)/select_n | solution.py:108
  190.9 2.0 fusion.41
  193.0 4.0 %all-to-all-start.1 = ((bf16[32,8,1024]{2,1,0:T(8,128)(2,1)}), bf16[32,8,1024]{2,1,0:T(8,128)(2,1)S(1)}, u32[]{:S(2)}, u32[]{:S(2)}) async-start(bf16[32,8,1024]{2,1,0:T(8,128)(2,1)} %fusion.41), calls=%async_computation.2 | async-start | bytes 1048576 | tf_op jit(solution)/shard_map/all_to_all | solution.py:172
  199.0 1.8 copy.49
  203.4 2.4 %copy.58 = f32[96,8,8,128]{3,1,2,0:T(8,128)} copy(f32[96,8,8,128]{3,2,1,0:T(8,128)S(1)} %bitcast.115) | data formatting | bytes 6291456
  (109 shorter events, 35.8 us)
Async XLA Ops:
  7.2 73.4 %copy-start = (bf16[1,1024,1024]{2,1,0:T(8,128)(2,1)S(1)}, bf16[1,1024,1024]{2,1,0:T(8,128)(2,1)}, u32[]{:S(2)}) copy-start(bf16[1,1024,1024]{2,1,0:T(8,128)(2,1)} %param.19) | copy-start | bytes 6291460
  8.1 21.7 %collective-permute-start = (bf16[4,1,512]{2,1,0:T(2,128)(2,1)S(1)}, bf16[4,1,512]{2,1,0:T(2,128)(2,1)S(1)}, u32[]{:S(2)}, u32[]{:S(2)}) collective-permute-start(bf16[4,1,512]{2,1,0:T(2,128)(2,1)S(1)} %get-tuple-element.42), channel_id=1, source_target_pairs={{0,1},{1,2},{2,3},{3,4},{4,5},{5,6},{6,7},{7,8},{8,9},{9,10},{10,1... | collective-permute-start | bytes 12296 | tf_op jit(solution)/shard_map/ppermute | solution.py:28
  12.1 17.7 %collective-permute-start.1 = (bf16[4,1,512]{2,1,0:T(2,128)(2,1)S(1)}, bf16[4,1,512]{2,1,0:T(2,128)(2,1)S(1)}, u32[]{:S(2)}, u32[]{:S(2)}) collective-permute-start(bf16[4,1,512]{2,1,0:T(2,128)(2,1)S(1)} %get-tuple-element.43), channel_id=1, source_target_pairs={{1,0},{2,1},{3,2},{4,3},{5,4},{6,5},{7,6},{8,7},{9,8},{10,9},{11,1... | collective-permute-start | bytes 12296 | tf_op jit(solution)/shard_map/ppermute | solution.py:29
  19.7 20.8 %all-to-all-start.2 = ((bf16[32,8,1024]{2,1,0:T(8,128)(2,1)}), bf16[32,8,1024]{2,1,0:T(8,128)(2,1)S(1)}, u32[]{:S(2)}, u32[]{:S(2)}) async-start(bf16[32,8,1024]{2,1,0:T(8,128)(2,1)} %fusion.31), calls=%async_computation.3 | async-start | bytes 1048576 | tf_op jit(solution)/shard_map/all_to_all | solution.py:138
  30.6 28.4 %copy-start.12 = (bf16[144,576]{1,0:T(8,128)(2,1)S(1)}, bf16[144,576]{1,0:T(8,128)(2,1)}, u32[]{:S(2)}) copy-start(bf16[144,576]{1,0:T(8,128)(2,1)} %constant.98.clone) | copy-start | bytes 497668
  40.4 5.6 %copy-start.10 = (bf16[32,8,1024]{2,1,0:T(8,128)(2,1)}, bf16[32,8,1024]{2,1,0:T(8,128)(2,1)S(1)}, u32[]{:S(2)}) copy-start(bf16[32,8,1024]{2,1,0:T(8,128)(2,1)S(1)} %all-to-all-done.2) | copy-start | bytes 1572868
  41.3 17.6 %all-to-all-start = ((bf16[128,8,144]{2,1,0:T(8,128)(2,1)}), bf16[128,8,144]{2,1,0:T(8,128)(2,1)}, u32[]{:S(2)}, u32[]{:S(2)}) async-start(bf16[128,8,144]{2,1,0:T(8,128)(2,1)} %bitcast.4), calls=%async_computation | async-start | bytes 1048576 | tf_op jit(solution)/shard_map/all_to_all | solution.py:146
  46.0 34.6 %all-gather.2.cloned.1.call-start = ((), (), s32[]{:S(2)}) async-start(), calls=%async_computation.7 | async-start | bytes 2621440 | tf_op jit(solution)/shard_map/all_gather | solution.py:141
  46.7 144.2 %reduce-scatter.2.cloned.1.call-start = ((), (), s32[]{:S(2)}) async-start(), calls=%async_computation.6 | async-start | bytes 2621440 | tf_op jit(solution)/shard_map/reduce_scatter | solution.py:169
  62.9 4.4 %copy-start.13 = (f32[1024]{0:T(1024)S(1)}, f32[1024]{0:T(1024)}, u32[]{:S(2)}) copy-start(f32[1024]{0:T(1024)} %param.15) | copy-start | bytes 12292
  67.3 2.1 copy-start.2
  67.3 3.1 %copy-start.14 = (bf16[1,1024,1024]{2,1,0:T(8,128)(2,1)S(1)}, bf16[1,1024,1024]{2,1,0:T(8,128)(2,1)}, u32[]{:S(2)}) copy-start(bf16[1,1024,1024]{2,1,0:T(8,128)(2,1)} %param.18) | copy-start | bytes 6291460
  69.4 5.4 %copy-start.5 = (bf16[1024,1024]{0,1:T(8,128)(2,1)}, bf16[1024,1024]{0,1:T(8,128)(2,1)S(1)}, u32[]{:S(2)}) copy-start(bf16[1024,1024]{0,1:T(8,128)(2,1)S(1)} %get-tuple-element.37) | copy-start | bytes 6291460
  70.5 4.4 %copy-start.16 = (bf16[1,1024,1024]{2,1,0:T(8,128)(2,1)S(1)}, bf16[1,1024,1024]{2,1,0:T(8,128)(2,1)}, u32[]{:S(2)}) copy-start(bf16[1,1024,1024]{2,1,0:T(8,128)(2,1)} %param.17) | copy-start | bytes 6291460
  80.6 8.5 %copy-start.15 = (bf16[1,1024,1024]{2,1,0:T(8,128)(2,1)S(1)}, bf16[1,1024,1024]{2,1,0:T(8,128)(2,1)}, u32[]{:S(2)}) copy-start(bf16[1,1024,1024]{2,1,0:T(8,128)(2,1)} %param.18) | copy-start | bytes 6291460
  89.0 2.4 %copy-start.21 = (bf16[1024,1024]{0,1:T(8,128)(2,1)}, bf16[1024,1024]{0,1:T(8,128)(2,1)S(1)}, u32[]{:S(2)}) copy-start(bf16[1024,1024]{0,1:T(8,128)(2,1)S(1)} %get-tuple-element.39) | copy-start | bytes 6291460
  89.1 3.6 %copy-start.18 = (bf16[1024,1024]{0,1:T(8,128)(2,1)}, bf16[1024,1024]{0,1:T(8,128)(2,1)S(1)}, u32[]{:S(2)}) copy-start(bf16[1024,1024]{0,1:T(8,128)(2,1)S(1)} %get-tuple-element.38) | copy-start | bytes 6291460
  89.1 3.1 %copy-start.6 = (bf16[1024,1024]{0,1:T(8,128)(2,1)S(1)}, bf16[1024,1024]{0,1:T(8,128)(2,1)}, u32[]{:S(2)}) copy-start(bf16[1024,1024]{0,1:T(8,128)(2,1)} %copy-done.5) | copy-start | bytes 6291460
  89.1 4.3 %copy-start.3 = (f32[1024,1024]{0,1:T(8,128)S(1)}, f32[1024,1024]{0,1:T(8,128)}, u32[]{:S(2)}) copy-start(f32[1024,1024]{0,1:T(8,128)} %copy-done.2) | copy-start | bytes 12582916
  89.1 4.9 %copy-start.17 = (bf16[1,1024,1024]{2,1,0:T(8,128)(2,1)S(1)}, bf16[1,1024,1024]{2,1,0:T(8,128)(2,1)}, u32[]{:S(2)}) copy-start(bf16[1,1024,1024]{2,1,0:T(8,128)(2,1)} %param.17) | copy-start | bytes 6291460
  97.2 2.2 %copy-start.8 = (f32[1024,768]{1,0:T(8,128)S(1)}, f32[1024,768]{1,0:T(8,128)}, u32[]{:S(2)}) copy-start(f32[1024,768]{1,0:T(8,128)} %fusion.33) | copy-start | bytes 9437188
  98.1 1.3 copy-start.11
  117.8 2.4 %copy-start.19 = (bf16[1024,1024]{0,1:T(8,128)(2,1)S(1)}, bf16[1024,1024]{0,1:T(8,128)(2,1)}, u32[]{:S(2)}) copy-start(bf16[1024,1024]{0,1:T(8,128)(2,1)} %get-tuple-element.35) | copy-start | bytes 6291460
  118.2 1.1 copy-start.4
  119.4 4.5 %collective-permute-start.2 = (bf16[64,56,128]{2,1,0:T(8,128)(2,1)S(1)}, bf16[64,56,128]{2,1,0:T(8,128)(2,1)}, u32[]{:S(2)}, u32[]{:S(2)}) collective-permute-start(bf16[64,56,128]{2,1,0:T(8,128)(2,1)S(1)} %fusion.37), channel_id=1, source_target_pairs={{0,4},{4,0},{1,5},{5,1},{2,6},{6,2},{3,7},{7,3},{8,12},{12,8},{9,1... | collective-permute-start | bytes 2752520 | tf_op jit(solution)/shard_map/ppermute | solution.py:94
  151.1 23.0 %all-to-all-start.4 = ((bf16[64,56,128]{2,1,0:T(8,128)(2,1)}), bf16[64,56,128]{2,1,0:T(8,128)(2,1)S(1)}, u32[]{:S(2)}, u32[]{:S(2)}) async-start(bf16[64,56,128]{2,1,0:T(8,128)(2,1)} %broadcast_in_dim.100), calls=%async_computation.5 | async-start | bytes 1835008 | tf_op jit(solution)/shard_map/all_to_all | solution.py:106
  174.1 10.0 %copy-start.7 = (bf16[64,56,128]{2,1,0:T(8,128)(2,1)}, bf16[64,56,128]{2,1,0:T(8,128)(2,1)S(1)}, u32[]{:S(2)}) copy-start(bf16[64,56,128]{2,1,0:T(8,128)(2,1)S(1)} %all-to-all-done.4) | copy-start | bytes 2752516
  174.1 10.0 %copy-start.9 = (bf16[1024,1024]{0,1:T(8,128)(2,1)S(1)}, bf16[1024,1024]{0,1:T(8,128)(2,1)}, u32[]{:S(2)}) copy-start(bf16[1024,1024]{0,1:T(8,128)(2,1)} %copy.43) | copy-start | bytes 6291460
  174.1 10.0 %copy-start.20 = (bf16[1024,1024]{0,1:T(8,128)(2,1)S(1)}, bf16[1024,1024]{0,1:T(8,128)(2,1)}, u32[]{:S(2)}) copy-start(bf16[1024,1024]{0,1:T(8,128)(2,1)} %get-tuple-element.35) | copy-start | bytes 6291460
  174.1 14.4 %collective-permute-start.3 = (bf16[64,56,128]{2,1,0:T(8,128)(2,1)S(1)}, bf16[64,56,128]{2,1,0:T(8,128)(2,1)S(1)}, u32[]{:S(2)}, u32[]{:S(2)}) collective-permute-start(bf16[64,56,128]{2,1,0:T(8,128)(2,1)S(1)} %all-to-all-done.4), channel_id=1, source_target_pairs={{0,4},{4,0},{1,5},{5,1},{2,6},{6,2},{3,7},{7,3},{8,12},{12,8},{9,1... | collective-permute-start | bytes 2752520 | tf_op jit(solution)/shard_map/ppermute | solution.py:94
  193.0 15.8 %all-to-all-start.1 = ((bf16[32,8,1024]{2,1,0:T(8,128)(2,1)}), bf16[32,8,1024]{2,1,0:T(8,128)(2,1)S(1)}, u32[]{:S(2)}, u32[]{:S(2)}) async-start(bf16[32,8,1024]{2,1,0:T(8,128)(2,1)} %fusion.41), calls=%async_computation.2 | async-start | bytes 1048576 | tf_op jit(solution)/shard_map/all_to_all | solution.py:172
  203.4 2.4 %copy-start.1 = (bf16[64,56,128]{2,1,0:T(8,128)(2,1)S(1)}, bf16[64,56,128]{2,1,0:T(8,128)(2,1)}, u32[]{:S(2)}) copy-start(bf16[64,56,128]{2,1,0:T(8,128)(2,1)} %get-tuple-element.41) | copy-start | bytes 2752516
Sparse Core Ops, SparseCore 0:
  48.5 32.0 all-gather.1
  124.1 39.3 reduce-scatter.1

commit v2 on v1

v2 whole, which is shorter than its diff:
```python
import jax
import jax.numpy as jnp
import numpy as np
from jax import lax
from jax.experimental import pallas as pl
from jax.experimental.pallas import tpu as pltpu
from jax.sharding import PartitionSpec as P

PATCH = 4
GELU_C = 0.7978845608028654
GELU_A = 0.044715
EPSILON = 1e-06
BF = jnp.bfloat16
F32 = jnp.float32
PIX = 144
DE = ("xz", "core")
ALL = ("tp", "xz", "core")
DE_TP = ("xz", "core", "tp")
HALF = ("xz", "tp")


def dot(a, b, dims=((1,), (0,))):
    return lax.dot_general(a, b, (dims, ((), ())), preferred_element_type=F32)


def halo_rows(raw):
    count = lax.axis_size(DE_TP)
    forward = [(i, i + 1) for i in range(count - 1)]
    backward = [(target, source) for source, target in forward]
    low = lax.ppermute(raw[:, -1:], DE_TP, forward)
    high = lax.ppermute(raw[:, :1], DE_TP, backward)
    return jnp.concatenate([low, raw, high], axis=1)


def window_rows(padded, tokens):
    chans, rows, cols = padded.shape
    flat = padded.reshape(chans * rows, cols)
    step = lax.broadcasted_iota(jnp.int32, (6, tokens, cols), 0)
    token = lax.broadcasted_iota(jnp.int32, (6, tokens, cols), 1)
    col = lax.broadcasted_iota(jnp.int32, (6, tokens, cols), 2)
    pick = (col == PATCH * token + step - 1).astype(BF)
    out = lax.dot_general(pick, flat, (((2,), (1,)), ((), ())), preferred_element_type=F32)
    return out.transpose(1, 0, 2).reshape(tokens, 6 * chans * rows).astype(BF)


def placement():
    place = np.zeros((6, 4, 6, 16, 4, 3, 3), np.float32)
    for r in range(4):
        for c in range(4):
            for a in range(3):
                for b in range(3):
                    for i in range(4):
                        place[c + b, i, r + a, r * 4 + c, i, a, b] = 1
    return place.reshape(PIX, 16 * 36)


TAPS = 40


def placement_rows():
    place = placement().T.reshape(16, 36, PIX)
    return np.pad(place, ((0, 0), (0, TAPS - 36), (0, 0))).reshape(16 * TAPS, PIX)


def front_kernel(
    cells_ref, conv_ref, embed_ref, gain_ref, router_ref, gate_ref, up_ref, down_ref,
    patches_ref, slope_ref, hidden_ref, normed_ref, inv_ref, score_ref, act_ref, silu_ref, fac_ref, out_ref,
):
    preact = dot(cells_ref[...], conv_ref[...])
    square = preact * preact
    tanh_v = jnp.tanh(GELU_C * (preact + GELU_A * square * preact))
    half = 0.5 * (1.0 + tanh_v)
    patches = (preact * half).astype(BF)
    patches_ref[...] = patches
    slope_ref[...] = half + 0.5 * preact * (1.0 - tanh_v * tanh_v) * GELU_C * (
        1.0 + 3.0 * GELU_A * square
    )
    embedded = dot(patches, embed_ref[...])
    inv_rms = lax.rsqrt(jnp.mean(embedded * embedded, axis=-1, keepdims=True) + EPSILON)
    inv_ref[...] = inv_rms
    normed = embedded * inv_rms
    normed_ref[...] = normed
    hidden = (normed * gain_ref[...]).astype(BF)
    hidden_ref[...] = hidden
    logit = jnp.sum(hidden.astype(F32) * router_ref[...], axis=1, keepdims=True)
    score_ref[...] = jax.nn.sigmoid(logit)
    gate_proj = dot(hidden, gate_ref[...])
    up_proj = dot(hidden, up_ref[...])
    sigmoid_gate = jax.nn.sigmoid(gate_proj)
    activated = gate_proj * sigmoid_gate
    silu_ref[...] = activated
    fac_ref[...] = up_proj * (sigmoid_gate * (1.0 + gate_proj * (1.0 - sigmoid_gate)))
    hidden_act = (activated * up_proj).astype(BF)
    act_ref[...] = hidden_act
    out_ref[...] = dot(hidden_act, down_ref[...]).astype(BF)


def whole(shape):
    return pl.BlockSpec(shape, lambda i: (0,) * len(shape), pipeline_mode=pl.Buffered(1))


def rows_of(block, width):
    return pl.BlockSpec((block, width), lambda i: (i, 0))


def front(cells, conv, embed_weight, gain, router_row, w_gate, w_up, w_down):
    total = cells.shape[0]
    pixels = conv.shape[1]
    width = embed_weight.shape[1]
    units = w_gate.shape[1]
    block = 256
    sizes = (
        (pixels, BF), (pixels, F32), (width, BF), (width, F32), (1, F32), (1, F32),
        (units, BF), (units, F32), (units, F32), (width, BF),
    )
    return pl.pallas_call(
        front_kernel,
        grid=(total // block,),
        in_specs=[
            rows_of(block, PIX), whole(conv.shape), whole(embed_weight.shape), whole(gain.shape),
            whole(router_row.shape), whole(w_gate.shape), whole(w_up.shape), whole(w_down.shape),
        ],
        out_specs=[rows_of(block, size) for size, _ in sizes],
        out_shape=[jax.ShapeDtypeStruct((total, size), kind) for size, kind in sizes],
        compiler_params=pltpu.CompilerParams(vmem_limit_bytes=48 << 20),
        cost_estimate=pl.CostEstimate(flops=8 << 30, bytes_accessed=32 << 20, transcendentals=0),
    )(cells, conv, embed_weight, gain, router_row, w_gate, w_up, w_down)


def back_kernel(
    expert_ref, cots_ref, silu_ref, fac_ref, act_ref, score_ref, normed_ref, inv_ref, hidden_ref, slope_ref,
    patches_ref, cells_ref, place_ref, router_ref, gain_ref, embed_ref, gate_ref, up_ref, down_ref,
    gate_cot_ref, up_cot_ref, out_cot_ref, pieces_ref,
    embed_cot_ref, preact_cot_ref, sums_ref,
):
    step = pl.program_id(0)
    block = cots_ref.shape[0]
    rows = pl.ds(pl.multiple_of(step * block, block), block)
    cot = cots_ref[...]
    act_raw = dot(cot, down_ref[...], ((1,), (1,)))
    score = score_ref[...]
    score_grad = jnp.sum(act_ref[...].astype(F32) * act_raw, axis=1, keepdims=True)
    logit_cot = score_grad * score * (1.0 - score)
    out_cot_ref[...] = (score * cot.astype(F32)).astype(BF)
    act_cot = score * act_raw
    gate_cot = (act_cot * fac_ref[...]).astype(BF)
    up_cot = (act_cot * silu_ref[...]).astype(BF)
    gate_cot_ref[...] = gate_cot
    up_cot_ref[...] = up_cot
    slot_cot = dot(gate_cot, gate_ref[...], ((1,), (1,))) + dot(up_cot, up_ref[...], ((1,), (1,)))
    upstream = slot_cot + logit_cot * router_ref[...]
    normed = normed_ref[...]
    scaled = upstream * gain_ref[...]
    product = upstream * normed
    mean = jnp.mean(product * gain_ref[...], axis=-1, keepdims=True)
    embed_cot = (inv_ref[...] * (scaled - normed * mean)).astype(BF)
    embed_cot_ref[rows, :] = embed_cot

    @pl.when(step == 0)
    def _():
        sums_ref[...] = jnp.zeros_like(sums_ref)

    sums_ref[0:1, :] += jnp.sum(hidden_ref[...].astype(F32) * logit_cot, axis=0, keepdims=True)
    sums_ref[1:2, :] += jnp.sum(product, axis=0, keepdims=True)
    feature_cot = dot(embed_cot, embed_ref[...], ((1,), (1,)))
    preact_cot_ref[rows, :] = (feature_cot * slope_ref[...]).astype(BF)

    @pl.when(step == pl.num_programs(0) - 1)
    def _():
        tall, lanes = 48, 128
        embed_part = dot(patches_ref[...], embed_cot_ref[...], ((0,), (0,)))
        across = embed_part.shape[1] // lanes
        for a in range(embed_part.shape[0] // tall):
            for b in range(across):
                pieces_ref[a * across + b, 0:tall, :] = embed_part[
                    a * tall : a * tall + tall, b * lanes : b * lanes + lanes
                ]
        product_sum = dot(cells_ref[...], preact_cot_ref[...], ((0,), (0,)))
        taps = dot(place_ref[...], product_sum.astype(BF))
        pixels = taps.shape[1]
        col = lax.broadcasted_iota(jnp.int32, (TAPS, pixels), 1)
        wide = jnp.zeros((TAPS, pixels), F32)
        for cell in range(16):
            wide += jnp.where(col % 16 == cell, taps[cell * TAPS : cell * TAPS + TAPS], 0.0)
        chan = lax.broadcasted_iota(jnp.int32, (lanes, pixels), 0)
        group = lax.broadcasted_iota(jnp.int32, (lanes, pixels), 1)
        stem = dot(wide.astype(BF), (chan == group // 16).astype(BF), ((1,), (1,)))

        def folded(row):
            return jnp.concatenate(
                [row[:, k * lanes : k * lanes + lanes] for k in range(across)], axis=0
            )

        router = folded(sums_ref[0:1, :])
        for e in range(32):
            pieces_ref[e, tall:, :] = jnp.where(expert_ref[0] == e, router, 0.0)
        pieces_ref[32, tall:, :] = folded(sums_ref[1:2, :])
        for k in range(5):
            pieces_ref[33 + k, tall:, :] = stem[8 * k : 8 * k + 8]
        for k in range(38, pieces_ref.shape[0]):
            pieces_ref[k, tall:, :] = jnp.zeros((8, lanes), F32)


def back(expert, cots, saved, cells, router_row, gain, embed_weight, w_gate, w_up, w_down):
    patches, slope, hidden, normed, inv_rms, score, hidden_act, silu, fac = saved
    total, width = cots.shape
    units = w_gate.shape[1]
    pixels = patches.shape[1]
    block = 256
    place = jnp.asarray(placement_rows(), BF)
    ins = (
        (expert, pl.BlockSpec(memory_space=pltpu.SMEM)),
        (cots, rows_of(block, width)),
        (silu, rows_of(block, units)),
        (fac, rows_of(block, units)),
        (hidden_act, rows_of(block, units)),
        (score, rows_of(block, 1)),
        (normed, rows_of(block, width)),
        (inv_rms, rows_of(block, 1)),
        (hidden, rows_of(block, width)),
        (slope, rows_of(block, pixels)),
        (patches, whole(patches.shape)),
        (cells, whole(cells.shape)),
        (place, whole(place.shape)),
        (router_row, whole(router_row.shape)),
        (gain, whole(gain.shape)),
        (embed_weight, whole(embed_weight.shape)),
        (w_gate, whole(w_gate.shape)),
        (w_up, whole(w_up.shape)),
        (w_down, whole(w_down.shape)),
    )
    return pl.pallas_call(
        back_kernel,
        grid=(total // block,),
        in_specs=[spec for _, spec in ins],
        out_specs=[rows_of(block, units), rows_of(block, units), rows_of(block, width), whole((128, 56, 128))],
        out_shape=[
            jax.ShapeDtypeStruct((total, units), BF),
            jax.ShapeDtypeStruct((total, units), BF),
            jax.ShapeDtypeStruct((total, width), BF),
            jax.ShapeDtypeStruct((128, 56, 128), F32),
        ],
        scratch_shapes=[
            pltpu.VMEM((total, width), BF),
            pltpu.VMEM((total, pixels), BF),
            pltpu.VMEM((8, width), F32),
        ],
        compiler_params=pltpu.CompilerParams(vmem_limit_bytes=56 << 20),
        cost_estimate=pl.CostEstimate(flops=10 << 30, bytes_accessed=36 << 20, transcendentals=0),
    )(*[x for x, _ in ins])


def finish_kernel(core_ref, mine_ref, theirs_ref, embed_ref, router_ref, gain_ref, stem_ref):
    first = core_ref[0] == 0
    count = mine_ref.shape[0]
    tall, lanes = 48, 128
    across = embed_ref.shape[1] // lanes

    def piece(p):
        near = mine_ref[p % count].astype(F32)
        far = theirs_ref[p % count].astype(F32)
        return jnp.where(first, near, far) if p < count else jnp.where(first, far, near)

    experts = router_ref.shape[1]
    rows = []
    for p in range(2 * count):
        value = piece(p)
        a, b = p // across, p % across
        embed_ref[a * tall : a * tall + tall, b * lanes : b * lanes + lanes] = value[:tall]
        if p < experts:
            rows.append(value[tall:])
        elif p == experts:
            gain_ref[...] = value[tall:]
        elif p < experts + 6:
            k = p - experts - 1
            stem_ref[8 * k : 8 * k + 8, :] = value[tall:]
    for k in range(across):
        block = jnp.concatenate([row[k : k + 1] for row in rows], axis=0)
        router_ref[k * lanes : k * lanes + lanes, :] = block.T


def finish(core, mine, theirs, pixels, width, experts):
    return pl.pallas_call(
        finish_kernel,
        in_specs=[
            pl.BlockSpec(memory_space=pltpu.SMEM),
            pl.BlockSpec(memory_space=pltpu.VMEM),
            pl.BlockSpec(memory_space=pltpu.VMEM),
        ],
        out_specs=[pl.BlockSpec(memory_space=pltpu.VMEM)] * 4,
        out_shape=[
            jax.ShapeDtypeStruct((pixels, width), F32),
            jax.ShapeDtypeStruct((width, experts), F32),
            jax.ShapeDtypeStruct((8, 128), F32),
            jax.ShapeDtypeStruct((TAPS, 128), F32),
        ],
        compiler_params=pltpu.CompilerParams(vmem_limit_bytes=32 << 20),
        cost_estimate=pl.CostEstimate(flops=1 << 20, bytes_accessed=6 << 20, transcendentals=0),
    )(core, mine, theirs)


def cell_mask(channels):
    cell = lax.broadcasted_iota(jnp.int32, (16, channels * 16), 0)
    col = lax.broadcasted_iota(jnp.int32, (16, channels * 16), 1)
    return cell == col % 16


def spread(channels):
    chan = lax.broadcasted_iota(jnp.int32, (channels, channels * 16), 0)
    col = lax.broadcasted_iota(jnp.int32, (channels, channels * 16), 1)
    return (chan == col // 16).astype(BF)


def stem_matrix(stem_weight):
    channels = stem_weight.shape[0]
    taps = stem_weight.reshape(channels, 36)
    wide = dot(taps, spread(channels), ((0,), (0,))).astype(BF)
    stack = jnp.where(cell_mask(channels)[:, None, :], wide[None], BF(0))
    return dot(jnp.asarray(placement(), BF), stack.reshape(16 * 36, channels * 16)).astype(BF)


def slots_of(route, experts, capacity):
    tokens = route.shape[0]
    hot = (route[:, None] == jnp.arange(experts, dtype=jnp.int32)[None, :]).astype(F32)
    row = lax.broadcasted_iota(jnp.int32, (tokens, tokens), 0)
    col = lax.broadcasted_iota(jnp.int32, (tokens, tokens), 1)
    before = dot((col < row).astype(BF), hot.astype(BF))
    return route * capacity + jnp.sum(before * hot, axis=1).astype(jnp.int32)


def swap(block):
    count = lax.axis_size("core")
    return lax.ppermute(block, "core", [(i, count - 1 - i) for i in range(count)])


def total_over_all(pieces, beside):
    count = pieces.shape[0] // 2
    core = lax.axis_index("core")
    own = lax.dynamic_slice_in_dim(pieces, core * count, count, axis=0)
    other = lax.dynamic_slice_in_dim(pieces, (1 - core) * count, count, axis=0)
    chip = (own + swap(other.astype(BF)).astype(F32)).astype(BF)
    parts = lax.all_to_all(chip, HALF, split_axis=0, concat_axis=0, tiled=True)
    parts, done = lax.optimization_barrier((parts, beside(chip)))
    total = jnp.sum(parts.astype(F32), axis=0).astype(BF)
    copies = jnp.broadcast_to(total[None], parts.shape)
    mine = lax.all_to_all(copies, HALF, split_axis=0, concat_axis=0, tiled=True)
    theirs = swap(mine)
    return mine, theirs, done


def local(
    raw_tiles,
    stem_weight,
    embed_weight,
    norm_gain,
    router_weight,
    w_gate,
    w_up,
    w_down,
    routes,
    cotangent,
):
    tokens, width = cotangent.shape
    owners = lax.axis_size(DE)
    members = lax.axis_size("tp")
    devices = owners * members
    experts = owners
    capacity = 2 * tokens // experts
    slots = experts * capacity
    total = devices * capacity
    w_gate, w_up, w_down = w_gate[0], w_up[0], w_down[0]

    slot_of = slots_of(routes[:, 0], experts, capacity)
    selector = (slot_of[None, :] == jnp.arange(slots, dtype=jnp.int32)[:, None]).astype(BF)
    sent_cots = dot(selector, cotangent).astype(BF)
    moved = lax.all_to_all(
        sent_cots.reshape(experts, capacity, width), DE, split_axis=0, concat_axis=0, tiled=True
    )
    windows = window_rows(halo_rows(raw_tiles), tokens)
    sent_windows = dot(selector, windows).astype(BF).reshape(1, experts, capacity, PIX)
    sent_windows, moved = lax.optimization_barrier((sent_windows, moved))
    sent_windows = jnp.broadcast_to(sent_windows, (members, experts, capacity, PIX))
    cells = lax.all_to_all(
        sent_windows.reshape(devices, capacity, PIX), ALL, split_axis=0, concat_axis=0, tiled=True
    ).reshape(total, PIX)

    cots = lax.all_gather(moved, "tp", axis=0, tiled=True).reshape(total, width)

    conv = stem_matrix(stem_weight)
    expert = lax.axis_index(DE)
    router_row = lax.dynamic_slice_in_dim(router_weight, expert, 1, axis=1).reshape(1, width)
    router_row = router_row.astype(F32)
    gain = norm_gain.reshape(1, width)
    *saved, out_part = front(cells, conv, embed_weight, gain, router_row, w_gate, w_up, w_down)
    hidden, score, hidden_act = saved[2], saved[5], saved[6]
    out_share = lax.psum_scatter(out_part, "tp", scatter_dimension=0, tiled=True)
    score_share = lax.dynamic_slice_in_dim(score, lax.axis_index("tp") * slots, slots, axis=0)
    mixed = (out_share.astype(F32) * score_share).astype(BF).reshape(experts, capacity, width)
    returned = lax.all_to_all(mixed, DE, split_axis=0, concat_axis=0, tiled=True)
    expert_mix = dot(selector, returned.reshape(slots, width), ((0,), (0,))).astype(BF)

    cots, out_part = lax.optimization_barrier((cots, out_part))
    gate_cot, up_cot, out_cot, pieces = back(
        expert.reshape(1), cots, saved, cells, router_row, gain, embed_weight, w_gate, w_up, w_down
    )

    def weight_grads(ready):
        rows, gates, ups, acts, outs, _ = lax.optimization_barrier(
            (hidden, gate_cot, up_cot, hidden_act, out_cot, ready)
        )
        return (
            dot(rows, gates, ((0,), (0,))),
            dot(rows, ups, ((0,), (0,))),
            dot(acts, outs, ((0,), (0,))),
        )

    mine, theirs, grads = total_over_all(pieces, weight_grads)
    core = lax.axis_index("core").reshape(1)
    embed_total, router_total, gain_total, stem_total = finish(
        core, mine, theirs, embed_weight.shape[0], width, experts
    )
    stem_total = stem_total[:36, : stem_weight.shape[0]].T
    return (
        expert_mix,
        grads[0][None],
        grads[1][None],
        grads[2][None],
        router_total,
        gain_total.reshape(width),
        embed_total,
        stem_total.reshape(stem_weight.shape),
    )


def solution(mesh):
    owners, members = mesh.devices.shape
    fine = jax.sharding.Mesh(mesh.devices.reshape(owners // 2, 2, members), ("xz", "core", "tp"))
    return jax.shard_map(
        local,
        mesh=fine,
        in_specs=(
            P(None, DE_TP, None),
            P(),
            P(),
            P(),
            P(),
            P(DE, None, "tp"),
            P(DE, None, "tp"),
            P(DE, "tp", None),
            P(DE_TP, None),
            P(DE_TP, None),
        ),
        out_specs=(
            P(DE_TP, None),
            P(DE, None, "tp"),
            P(DE, None, "tp"),
            P(DE, "tp", None),
            P(),
            P(),
            P(),
            P(),
        ),
        check_vma=False,
    )
```

time: 221 us -> 193 us (0.87); the launches traced: 217 us -> 192 us
  matrix products: 68.8 us -> 20.9 us
  Pallas kernels: 0 us -> 44.6 us
  local copies, waits for them, and re-layouts: 28.2 us -> 11.7 us
  waiting for transfers between devices: 26.7 us -> 37 us
  blocking collectives: 24.2 us -> 14.6 us
  other arithmetic: 15.3 us -> 6.27 us
  starting transfers between devices: 38.7 us -> 42.7 us
    dot_general x20 -> x9, matrix products: 68.3 us -> 20.4 us  [dot(): return lax.dot_general(a, b, (dims, ((), ())), preferred_element_type=F32)]
    pallas_call x0 -> x3, Pallas kernels: none -> 44.6 us  [the longest x1 25.4 us: back(): pl.pallas_call(back_kernel, grid=(total // block,), in_specs=[spec for _,...]
    all_to_all x1, waiting for transfers between devices: 4.29 us -> 14.3 us  [total_over_all(): mine = lax.all_to_all(copies, HALF, split_axis=0, concat_axis=0, tiled=True)]
    all_to_all x1, blocking collectives: 24.2 us -> 14.6 us  [local(): lax.all_to_all(mixed, DE, split_axis=0, concat_axis=0, tiled=True)]
    unnamed x50 -> x35, local copies, waits for them, and re-layouts: 14.5 us -> 5.08 us
    reshape x4 -> x0, local copies, waits for them, and re-layouts: 7.28 us -> none  [the longest x1 3.96 us: local(): cots = lax.all_gather(moved, 'tp', axis=0, tiled=True).reshape(total, width)]
    all_to_all x1, starting transfers between devices: 4.66 us -> 8.17 us  [local(): lax.all_to_all(sent_windows.reshape(devices, capacity, PIX), ALL, split_a...]
    reduce_sum x3 -> x0, other arithmetic: 2.9 us -> none  [the longest x1 1.73 us: stem_gather(): jnp.sum(jnp.where(cell_mask(channels)[:, None, :], cells, 0.0), axis=0)]
  transfers between devices with their start and end apart: 10 -> 10, of which waited for: 5 -> 5; matrix products, arithmetic and copies ran while one was open for 31% -> 17% of each run, Pallas kernels for 0% -> 22%
where the time goes in v2:
time: 193 us; the launch traced here: 192 us
  Pallas kernels  44.6 us (23%)
  starting transfers between devices  42.7 us (22%)
  waiting for transfers between devices  37 us (19%)
  matrix products  20.9 us (11%)
  blocking collectives  14.6 us (8%)
  between operations  14.3 us (7%)
  local copies, waits for them, and re-layouts  11.7 us (6%)
  other arithmetic  6.27 us (3%)
    pallas_call x1, Pallas kernels, back(): pl.pallas_call(back_kernel, grid=(total // block,), in_specs=[spec for _,...  25.4 us
    dot_general x9, matrix products, dot(): return lax.dot_general(a, b, (dims, ((), ())), preferred_element_type=F32)  20.4 us
    pallas_call x1, Pallas kernels, front(): pl.pallas_call(front_kernel, grid=(total // block,), in_specs=[rows_of(bl...  17.1 us
    all_to_all x1, blocking collectives, local(): lax.all_to_all(mixed, DE, split_axis=0, concat_axis=0, tiled=True)  14.6 us
    all_to_all x1, waiting for transfers between devices, total_over_all(): mine = lax.all_to_all(copies, HALF, split_axis=0, concat_axis=0, tiled=True)  14.3 us
    all_to_all x1, waiting for transfers between devices, local(): lax.all_to_all(sent_windows.reshape(devices, capacity, PIX), ALL, split_a...  10.2 us
    all_to_all x1, waiting for transfers between devices, local(): lax.all_to_all(sent_cots.reshape(experts, capacity, width), DE, split_axi...  9.98 us
    all_to_all x1, starting transfers between devices, total_over_all(): mine = lax.all_to_all(copies, HALF, split_axis=0, concat_axis=0, tiled=True)  9.5 us
  transfers between devices with their start and end apart: 10, of which 5 were waited for; matrix products, arithmetic and copies ran while one was open for 17% of the time, Pallas kernels for 22%

profile of v2, /device:TPU:1, one launch (start us, length us, event | category | flops | bytes accessed | tf_op | source)
XLA Modules:
  0.0 192.0 jit_solution(14542131435382234122)
XLA Ops:
  8.0 6.0 %collective-permute-start.1 = (bf16[4,1,512]{2,1,0:T(2,128)(2,1)S(1)}, bf16[4,1,512]{2,1,0:T(2,128)(2,1)S(1)}, u32[]{:S(2)}, u32[]{:S(2)}) collective-permute-start(bf16[4,1,512]{2,1,0:T(2,128)(2,1)S(1)} %get-tuple-element.93), channel_id=1, source_target_pairs={{1,0},{2,1},{3,2},{4,3},{5,4},{6,5},{7,6},{8,7},{9,8},{10,9},{11,1... | collective-permute-start | bytes 12296 | tf_op jit(solution)/shard_map/ppermute | solution.py:31
  14.0 1.9 %collective-permute-start = (bf16[4,1,512]{2,1,0:T(2,128)(2,1)S(1)}, bf16[4,1,512]{2,1,0:T(2,128)(2,1)S(1)}, u32[]{:S(2)}, u32[]{:S(2)}) collective-permute-start(bf16[4,1,512]{2,1,0:T(2,128)(2,1)S(1)} %get-tuple-element.92), channel_id=1, source_target_pairs={{0,1},{1,2},{2,3},{3,4},{4,5},{5,6},{6,7},{7,8},{8,9},{9,10},{10,1... | collective-permute-start | bytes 12296 | tf_op jit(solution)/shard_map/ppermute | solution.py:30
  16.0 0.9 fusion.5
  17.5 1.1 fusion.1
  18.6 8.0 %all-to-all-start = ((bf16[32,8,1024]{2,1,0:T(8,128)(2,1)}), bf16[32,8,1024]{2,1,0:T(8,128)(2,1)S(1)}, u32[]{:S(2)}, u32[]{:S(2)}) async-start(bf16[32,8,1024]{2,1,0:T(8,128)(2,1)} %fusion.1), calls=%async_computation | async-start | bytes 1048576 | tf_op jit(solution)/shard_map/all_to_all | solution.py:376
  28.3 10.0 %all-to-all-done = bf16[32,8,1024]{2,1,0:T(8,128)(2,1)S(1)} async-done(((bf16[32,8,1024]{2,1,0:T(8,128)(2,1)}), bf16[32,8,1024]{2,1,0:T(8,128)(2,1)S(1)}, u32[]{:S(2)}, u32[]{:S(2)}) %all-to-all-start) | async-done | bytes 524320 | tf_op jit(solution)/shard_map/all_to_all | solution.py:376
  39.5 0.8 broadcast_in_dim.48
  40.4 8.2 %all-to-all-start.1 = ((bf16[128,8,144]{2,1,0:T(8,128)(2,1)}), bf16[128,8,144]{2,1,0:T(8,128)(2,1)S(1)}, u32[]{:S(2)}, u32[]{:S(2)}) async-start(bf16[128,8,144]{2,1,0:T(8,128)(2,1)} %bitcast.56), calls=%async_computation.1 | async-start | bytes 1048576 | tf_op jit(solution)/shard_map/all_to_all | solution.py:383
  49.3 1.1 select_n.39
  50.4 1.5 fusion.2.conv_ref
  51.9 10.2 %all-to-all-done.1 = bf16[128,8,144]{2,1,0:T(8,128)(2,1)S(1)} async-done(((bf16[128,8,144]{2,1,0:T(8,128)(2,1)}), bf16[128,8,144]{2,1,0:T(8,128)(2,1)S(1)}, u32[]{:S(2)}, u32[]{:S(2)}) %all-to-all-start.1) | async-done | bytes 294944 | tf_op jit(solution)/shard_map/all_to_all | solution.py:383
  62.1 17.1 %shard_map.179 = (bf16[1024,768]{1,0:T(8,128)(2,1)S(1)}, f32[1024,768]{1,0:T(8,128)}, bf16[1024,1024]{1,0:T(8,128)(2,1)}, f32[1024,1024]{1,0:T(8,128)}, f32[1024...) custom-call(bf16[1024,144]{1,0:T(8,128)(2,1)S(1)} %bitcast.52, ...), custom_call_target="tpu_custom_call" | custom-call | flops 8589934592 | bytes 33554432 | tf_op jit(solution)/shard_map/pallas_call | solution.py:116
  80.1 1.2 copy-done.7
  82.1 25.4 %shard_map.180 = (bf16[1024,1024]{1,0:T(8,128)(2,1)}, bf16[1024,1024]{1,0:T(8,128)(2,1)}, bf16[1024,1024]{1,0:T(8,128)(2,1)}, f32[128,56,128]{2,1,0:T(8,128)}) custom-call(s32[1]{0:T(128)} %bitcast.17.expert_ref, bf16[1024,1024]{1,0:T(8,128)(2,1)} %bitcast.65, f32[1024,1024]{1,0:T(8,128)} %get-tuple-element.43.silu_ref, ...), custom_call_target="tpu_custom_call" | custom-call | flops 10737418240 | bytes 37748736 | tf_op jit(solution)/shard_map/pallas_call | solution.py:232
  107.5 1.6 dynamic-slice_convert_fusion
  109.1 1.3 collective-permute-start.2
  110.4 2.1 %collective-permute-done.2 = bf16[64,56,128]{2,1,0:T(8,128)(2,1)S(1)} collective-permute-done((bf16[64,56,128]{2,1,0:T(8,128)(2,1)S(1)}, bf16[64,56,128]{2,1,0:T(8,128)(2,1)S(1)}, u32[]{:S(2)}, u32[]{:S(2)}) %collective-permute-start.2) | collective-permute-done | bytes 917536 | tf_op jit(solution)/shard_map/ppermute | solution.py:333
  112.5 2.6 %add_convert_fusion = bf16[64,56,128]{2,1,0:T(8,128)(2,1)} fusion(bf16[64,56,128]{2,1,0:T(8,128)(2,1)S(1)} %collective-permute-done.2, f32[128,56,128]{2,1,0:T(8,128)} %get-tuple-element.51, s32[]{:T(128)S(6)} %select_n.42), kind=kLoop, calls=%fused_computation | loop fusion | flops 1376256 | bytes 3670020 | tf_op jit(solution)/shard_map/convert_element_type | solution.py:341
  115.1 4.8 %all-to-all-start.3 = ((bf16[64,56,128]{2,1,0:T(8,128)(2,1)}), bf16[64,56,128]{2,1,0:T(8,128)(2,1)S(1)}, u32[]{:S(2)}, u32[]{:S(2)}) async-start(bf16[64,56,128]{2,1,0:T(8,128)(2,1)} %add_convert_fusion), calls=%async_computation.4 | async-start | bytes 1835008 | tf_op jit(solution)/shard_map/all_to_all | solution.py:342
  120.0 6.8 %fusion.25 = f32[1024,1024]{1,0:T(8,128)} fusion(bf16[1024,1024]{1,0:T(8,128)(2,1)} %get-tuple-element.55.hidden_ref, bf16[1024,1024]{1,0:T(8,128)(2,1)} %get-tuple-element.56), kind=kOutput, calls=%fused_computation.52 | convolution fusion | flops 2147483648 | bytes 8388608 | tf_op jit(solution)/shard_map/dot_general | solution.py:23
  126.8 4.4 %fusion.26 = f32[1024,1024]{1,0:T(8,128)} fusion(bf16[1024,1024]{1,0:T(8,128)(2,1)S(1)} %copy-done.13, bf16[1024,1024]{1,0:T(8,128)(2,1)S(1)} %copy-done.15), kind=kOutput, calls=%fused_computation.53 | convolution fusion | flops 2147483648 | bytes 8388608 | tf_op jit(solution)/shard_map/dot_general | solution.py:23
  131.2 4.4 %fusion.27 = f32[1024,1024]{1,0:T(8,128)} fusion(bf16[1024,1024]{1,0:T(8,128)(2,1)S(1)} %copy-done.12, bf16[1024,1024]{1,0:T(8,128)(2,1)S(1)} %copy-done.14), kind=kOutput, calls=%fused_computation.54 | convolution fusion | flops 2147483648 | bytes 8388608 | tf_op jit(solution)/shard_map/dot_general | solution.py:23
  136.1 1.0 broadcast_in_dim.55
  137.1 9.5 %all-to-all-start.4 = ((bf16[64,56,128]{2,1,0:T(8,128)(2,1)}), bf16[64,56,128]{2,1,0:T(8,128)(2,1)S(1)}, u32[]{:S(2)}, u32[]{:S(2)}) async-start(bf16[64,56,128]{2,1,0:T(8,128)(2,1)} %broadcast_in_dim.55), calls=%async_computation.5 | async-start | bytes 1835008 | tf_op jit(solution)/shard_map/all_to_all | solution.py:346
  146.6 1.0 dynamic-slice_reduce_fusion
  147.7 14.3 %all-to-all-done.4.mine_ref = bf16[64,56,128]{2,1,0:T(8,128)(2,1)S(1)} async-done(((bf16[64,56,128]{2,1,0:T(8,128)(2,1)}), bf16[64,56,128]{2,1,0:T(8,128)(2,1)S(1)}, u32[]{:S(2)}, u32[]{:S(2)}) %all-to-all-start.4) | async-done | bytes 917536 | tf_op jit(solution)/shard_map/all_to_all | solution.py:346
  162.0 2.8 %collective-permute-start.3 = (bf16[64,56,128]{2,1,0:T(8,128)(2,1)S(1)}, bf16[64,56,128]{2,1,0:T(8,128)(2,1)S(1)}, u32[]{:S(2)}, u32[]{:S(2)}) collective-permute-start(bf16[64,56,128]{2,1,0:T(8,128)(2,1)S(1)} %all-to-all-done.4.mine_ref), channel_id=1, source_target_pairs={{0,4},{4,0},{1,5},{5,1},{2,6},{6,2},{3,7},{7,3},{8,12},{12,8},{9,1... | collective-permute-start | bytes 2752520 | tf_op jit(solution)/shard_map/ppermute | solution.py:333
  164.8 1.2 fusion.8
  166.0 14.6 %all_to_all.25 = bf16[32,8,1024]{2,1,0:T(8,128)(2,1)S(1)} all-to-all(bf16[32,8,1024]{2,1,0:T(8,128)(2,1)S(1)} %fusion.8), channel_id=1, replica_groups=mesh['xz'=16,'core'=2,'tp'=4] {'xz','core'}, dimensions={0} | all-to-all | bytes 1048576 | tf_op jit(solution)/shard_map/all_to_all | solution.py:399
  180.6 1.0 convolution_convert_fusion.1
  181.6 2.1 %shard_map.181 = (f32[768,1024]{1,0:T(8,128)}, f32[1024,32]{1,0:T(8,128)S(1)}, f32[8,128]{1,0:T(8,128)}, f32[40,128]{1,0:T(8,128)S(1)}) custom-call(s32[1]{0:T(128)} %bitcast.23.core_ref, bf16[64,56,128]{2,1,0:T(8,128)(2,1)S(1)} %all-to-all-done.4.mine_ref, bf16[64,56,128]{2,1,0:T(8,128)(2,1)S(1)} %collective-permute-done.3.theirs_ref), custom_call_target="tpu_custom_call" | custom-call | flops 1048576 | bytes 6291456 | tf_op jit(solution)/shard_map/pallas_call | solution.py:283
  183.7 0.8 copy.29
  (63 shorter events, 7.7 us)
Async XLA Ops:
  7.2 10.4 %copy-start = (bf16[128,1024]{1,0:T(8,128)(2,1)S(1)}, bf16[128,1024]{1,0:T(8,128)(2,1)}, u32[]{:S(2)}) copy-start(bf16[128,1024]{1,0:T(8,128)(2,1)} %param.21) | copy-start | bytes 786436
  7.2 32.0 %copy-start.11 = (bf16[48,4,3,3]{0,1,3,2:T(4,128)(2,1)S(1)}, bf16[48,4,3,3]{0,1,3,2:T(4,128)(2,1)}, u32[]{:S(2)}) copy-start(bf16[48,4,3,3]{0,1,3,2:T(4,128)(2,1)} %param.13) | copy-start | bytes 10372
  8.0 18.7 %collective-permute-start.1 = (bf16[4,1,512]{2,1,0:T(2,128)(2,1)S(1)}, bf16[4,1,512]{2,1,0:T(2,128)(2,1)S(1)}, u32[]{:S(2)}, u32[]{:S(2)}) collective-permute-start(bf16[4,1,512]{2,1,0:T(2,128)(2,1)S(1)} %get-tuple-element.93), channel_id=1, source_target_pairs={{1,0},{2,1},{3,2},{4,3},{5,4},{6,5},{7,6},{8,7},{9,8},{10,9},{11,1... | collective-permute-start | bytes 12296 | tf_op jit(solution)/shard_map/ppermute | solution.py:31
  14.0 12.7 %collective-permute-start = (bf16[4,1,512]{2,1,0:T(2,128)(2,1)S(1)}, bf16[4,1,512]{2,1,0:T(2,128)(2,1)S(1)}, u32[]{:S(2)}, u32[]{:S(2)}) collective-permute-start(bf16[4,1,512]{2,1,0:T(2,128)(2,1)S(1)} %get-tuple-element.92), channel_id=1, source_target_pairs={{0,1},{1,2},{2,3},{3,4},{4,5},{5,6},{6,7},{7,8},{8,9},{9,10},{10,1... | collective-permute-start | bytes 12296 | tf_op jit(solution)/shard_map/ppermute | solution.py:30
  18.6 19.7 %all-to-all-start = ((bf16[32,8,1024]{2,1,0:T(8,128)(2,1)}), bf16[32,8,1024]{2,1,0:T(8,128)(2,1)S(1)}, u32[]{:S(2)}, u32[]{:S(2)}) async-start(bf16[32,8,1024]{2,1,0:T(8,128)(2,1)} %fusion.1), calls=%async_computation | async-start | bytes 1048576 | tf_op jit(solution)/shard_map/all_to_all | solution.py:376
  26.7 55.4 %all-gather.2.cloned.1.call-start = ((), (), s32[]{:S(2)}) async-start(), calls=%async_computation.7 | async-start | bytes 2621440 | tf_op jit(solution)/shard_map/all_gather | solution.py:387
  38.3 0.8 copy-start.9
  39.4 11.0 %copy-start.10 = (bf16[144,576]{1,0:T(8,128)(2,1)S(1)}, bf16[144,576]{1,0:T(8,128)(2,1)}, u32[]{:S(2)}) copy-start(bf16[144,576]{1,0:T(8,128)(2,1)} %constant.76.clone) | copy-start | bytes 497668
  40.4 21.8 %copy-start.5 = (bf16[768,1024]{1,0:T(8,128)(2,1)S(1)}, bf16[768,1024]{1,0:T(8,128)(2,1)}, u32[]{:S(2)}) copy-start(bf16[768,1024]{1,0:T(8,128)(2,1)} %embed_ref.3) | copy-start | bytes 4718596
  40.4 21.8 %copy-start.6 = (f32[1024]{0:T(1024)S(1)}, f32[1024]{0:T(1024)}, u32[]{:S(2)}) copy-start(f32[1024]{0:T(1024)} %param.15) | copy-start | bytes 12292
  40.4 21.8 %all-to-all-start.1 = ((bf16[128,8,144]{2,1,0:T(8,128)(2,1)}), bf16[128,8,144]{2,1,0:T(8,128)(2,1)S(1)}, u32[]{:S(2)}, u32[]{:S(2)}) async-start(bf16[128,8,144]{2,1,0:T(8,128)(2,1)} %bitcast.56), calls=%async_computation.1 | async-start | bytes 1048576 | tf_op jit(solution)/shard_map/all_to_all | solution.py:383
  48.5 116.3 %reduce-scatter.2.cloned.1.call-start = ((), (), s32[]{:S(2)}) async-start(), calls=%async_computation.6 | async-start | bytes 2621440 | tf_op jit(solution)/shard_map/reduce_scatter | solution.py:396
  49.3 29.9 %copy-start.4 = (f32[1,1024]{1,0:T(1,128)}, f32[1,1024]{1,0:T(1,128)S(1)}, u32[]{:S(2)}) copy-start(f32[1,1024]{1,0:T(1,128)S(1)} %bitcast_convert_fusion.router_ref) | copy-start | bytes 12292
  62.1 17.1 %copy-start.2 = (bf16[128,8,144]{2,1,0:T(8,128)(2,1)}, bf16[128,8,144]{2,1,0:T(8,128)(2,1)S(1)}, u32[]{:S(2)}) copy-start(bf16[128,8,144]{2,1,0:T(8,128)(2,1)S(1)} %all-to-all-done.1) | copy-start | bytes 884740
  79.2 0.8 copy-start.3
  80.0 1.2 copy-start.7
  81.2 0.8 copy-start.8
  109.1 3.4 %collective-permute-start.2 = (bf16[64,56,128]{2,1,0:T(8,128)(2,1)S(1)}, bf16[64,56,128]{2,1,0:T(8,128)(2,1)S(1)}, u32[]{:S(2)}, u32[]{:S(2)}) collective-permute-start(bf16[64,56,128]{2,1,0:T(8,128)(2,1)S(1)} %dynamic-slice_convert_fusion), channel_id=1, source_target_pairs={{0,4},{4,0},{1,5},{5,1},{2,6},{6,2},{3,7},{7,3},{8,12},{12,8},{9,1... | collective-permute-start | bytes 2752520 | tf_op jit(solution)/shard_map/ppermute | solution.py:333
  115.1 20.8 %all-to-all-start.3 = ((bf16[64,56,128]{2,1,0:T(8,128)(2,1)}), bf16[64,56,128]{2,1,0:T(8,128)(2,1)S(1)}, u32[]{:S(2)}, u32[]{:S(2)}) async-start(bf16[64,56,128]{2,1,0:T(8,128)(2,1)} %add_convert_fusion), calls=%async_computation.4 | async-start | bytes 1835008 | tf_op jit(solution)/shard_map/all_to_all | solution.py:342
  120.0 6.8 %copy-start.13 = (bf16[1024,1024]{1,0:T(8,128)(2,1)S(1)}, bf16[1024,1024]{1,0:T(8,128)(2,1)}, u32[]{:S(2)}) copy-start(bf16[1024,1024]{1,0:T(8,128)(2,1)} %get-tuple-element.55.hidden_ref) | copy-start | bytes 6291460
  120.0 6.8 %copy-start.15 = (bf16[1024,1024]{1,0:T(8,128)(2,1)S(1)}, bf16[1024,1024]{1,0:T(8,128)(2,1)}, u32[]{:S(2)}) copy-start(bf16[1024,1024]{1,0:T(8,128)(2,1)} %get-tuple-element.57) | copy-start | bytes 6291460
  126.7 4.5 %copy-start.12 = (bf16[1024,1024]{1,0:T(8,128)(2,1)S(1)}, bf16[1024,1024]{1,0:T(8,128)(2,1)}, u32[]{:S(2)}) copy-start(bf16[1024,1024]{1,0:T(8,128)(2,1)} %get-tuple-element.58.act_ref) | copy-start | bytes 6291460
  126.8 4.5 %copy-start.14 = (bf16[1024,1024]{1,0:T(8,128)(2,1)S(1)}, bf16[1024,1024]{1,0:T(8,128)(2,1)}, u32[]{:S(2)}) copy-start(bf16[1024,1024]{1,0:T(8,128)(2,1)} %get-tuple-element.59) | copy-start | bytes 6291460
  137.1 24.9 %all-to-all-start.4 = ((bf16[64,56,128]{2,1,0:T(8,128)(2,1)}), bf16[64,56,128]{2,1,0:T(8,128)(2,1)S(1)}, u32[]{:S(2)}, u32[]{:S(2)}) async-start(bf16[64,56,128]{2,1,0:T(8,128)(2,1)} %broadcast_in_dim.55), calls=%async_computation.5 | async-start | bytes 1835008 | tf_op jit(solution)/shard_map/all_to_all | solution.py:346
  162.0 19.6 %collective-permute-start.3 = (bf16[64,56,128]{2,1,0:T(8,128)(2,1)S(1)}, bf16[64,56,128]{2,1,0:T(8,128)(2,1)S(1)}, u32[]{:S(2)}, u32[]{:S(2)}) collective-permute-start(bf16[64,56,128]{2,1,0:T(8,128)(2,1)S(1)} %all-to-all-done.4.mine_ref), channel_id=1, source_target_pairs={{0,4},{4,0},{1,5},{5,1},{2,6},{6,2},{3,7},{7,3},{8,12},{12,8},{9,1... | collective-permute-start | bytes 2752520 | tf_op jit(solution)/shard_map/ppermute | solution.py:333
  164.8 20.4 %copy-start.1 = (bf16[128,1024]{1,0:T(8,128)(2,1)S(1)}, bf16[128,1024]{1,0:T(8,128)(2,1)}, u32[]{:S(2)}) copy-start(bf16[128,1024]{1,0:T(8,128)(2,1)} %param.21) | copy-start | bytes 786436
Sparse Core Ops, SparseCore 0:
  39.3 35.4 all-gather.1
  82.2 26.3 reduce-scatter.1

commit v3 on v1

v3 whole, which is shorter than its diff:
```python
import jax
import jax.numpy as jnp
import numpy as np
from jax import lax
from jax.experimental import pallas as pl
from jax.experimental.pallas import tpu as pltpu
from jax.sharding import PartitionSpec as P

PATCH = 4
GELU_C = 0.7978845608028654
GELU_A = 0.044715
EPSILON = 1e-06
BF = jnp.bfloat16
F32 = jnp.float32
PIX = 144
DE = ("xz", "core")
ALL = ("tp", "xz", "core")
DE_TP = ("xz", "core", "tp")
HALF = ("xz", "tp")


def dot(a, b, dims=((1,), (0,))):
    return lax.dot_general(a, b, (dims, ((), ())), preferred_element_type=F32)


def halo_rows(raw):
    count = lax.axis_size(DE_TP)
    forward = [(i, i + 1) for i in range(count - 1)]
    backward = [(target, source) for source, target in forward]
    low = lax.ppermute(raw[:, -1:], DE_TP, forward)
    high = lax.ppermute(raw[:, :1], DE_TP, backward)
    return jnp.concatenate([low, raw, high], axis=1)


def window_rows(padded, tokens):
    chans, rows, cols = padded.shape
    flat = padded.reshape(chans * rows, cols)
    step = lax.broadcasted_iota(jnp.int32, (6, tokens, cols), 0)
    token = lax.broadcasted_iota(jnp.int32, (6, tokens, cols), 1)
    col = lax.broadcasted_iota(jnp.int32, (6, tokens, cols), 2)
    pick = (col == PATCH * token + step - 1).astype(BF)
    out = lax.dot_general(pick, flat, (((2,), (1,)), ((), ())), preferred_element_type=F32)
    return out.transpose(1, 0, 2).reshape(tokens, 6 * chans * rows).astype(BF)


def placement():
    place = np.zeros((6, 4, 6, 16, 4, 3, 3), np.float32)
    for r in range(4):
        for c in range(4):
            for a in range(3):
                for b in range(3):
                    for i in range(4):
                        place[c + b, i, r + a, r * 4 + c, i, a, b] = 1
    return place.reshape(PIX, 16 * 36)


TAPS = 40


def placement_rows():
    place = placement().T.reshape(16, 36, PIX)
    return np.pad(place, ((0, 0), (0, TAPS - 36), (0, 0))).reshape(16 * TAPS, PIX)


VMEM = pl.BlockSpec(memory_space=pltpu.VMEM)
SMEM = pl.BlockSpec(memory_space=pltpu.SMEM)
HBM = pl.BlockSpec(memory_space=pl.ANY)
ROWS = 256
TALL, LANES = 48, 128


def folded(row):
    return jnp.concatenate([row[:, k : k + LANES] for k in range(0, row.shape[1], LANES)], axis=0)


def layer_kernel(
    place_at_ref, gain_ref, router_ref, moved_hbm, conv_hbm, embed_hbm, gate_hbm, up_hbm, down_hbm, place_hbm,
    out_hbm, hidden_hbm, act_hbm, gate_cot_hbm, up_cot_hbm, out_cot_hbm, own_ref, other_ref,
    cells_ref, conv_ref, embed_ref, gate_ref, up_ref, down_ref, cots_ref, place_ref,
    out_ref, hidden_ref, act_ref, gate_cot_ref, up_cot_ref, out_cot_ref, patches_ref, embed_cot_ref, preact_cot_ref,
    in_sems, out_sems,
):
    total, width = cots_ref.shape
    pixels = patches_ref.shape[1]
    across = width // LANES
    arriving = {}
    for k, (name, source, target) in enumerate(
        (
            ("cells", moved_hbm.at[:, width:], cells_ref),
            ("conv", conv_hbm, conv_ref),
            ("embed", embed_hbm, embed_ref),
            ("gate", gate_hbm, gate_ref),
            ("up", up_hbm, up_ref),
            ("down", down_hbm, down_ref),
            ("cots", moved_hbm.at[:, :width], cots_ref),
            ("place", place_hbm, place_ref),
        )
    ):
        arriving[name] = pltpu.make_async_copy(source, target, in_sems.at[k])
        arriving[name].start()

    def need(name):
        if name in arriving:
            arriving.pop(name).wait()

    leaving = []

    def send(rows, k, source, target):
        leaving.append(pltpu.make_async_copy(source.at[rows], target.at[rows], out_sems.at[rows.start // ROWS, k]))
        leaving[-1].start()

    router_sum = jnp.zeros((1, width), F32)
    gain_sum = jnp.zeros((1, width), F32)
    for first in range(0, total, ROWS):
        rows = slice(first, first + ROWS)
        need("cells")
        need("conv")
        preact = dot(cells_ref[rows], conv_ref[...])
        square = preact * preact
        tanh_v = jnp.tanh(GELU_C * (preact + GELU_A * square * preact))
        half = 0.5 * (1.0 + tanh_v)
        patches = (preact * half).astype(BF)
        patches_ref[rows] = patches
        slope = half + 0.5 * preact * (1.0 - tanh_v * tanh_v) * GELU_C * (1.0 + 3.0 * GELU_A * square)
        need("embed")
        embedded = dot(patches, embed_ref[...])
        inv_rms = lax.rsqrt(jnp.mean(embedded * embedded, axis=-1, keepdims=True) + EPSILON)
        normed = embedded * inv_rms
        hidden = (normed * gain_ref[...]).astype(BF)
        hidden_ref[rows] = hidden
        send(rows, 0, hidden_ref, hidden_hbm)
        logit = jnp.sum(hidden.astype(F32) * router_ref[...], axis=1, keepdims=True)
        score = jax.nn.sigmoid(logit)
        need("gate")
        gate_proj = dot(hidden, gate_ref[...])
        need("up")
        up_proj = dot(hidden, up_ref[...])
        sigmoid_gate = jax.nn.sigmoid(gate_proj)
        activated = gate_proj * sigmoid_gate
        factor = up_proj * (sigmoid_gate * (1.0 + gate_proj * (1.0 - sigmoid_gate)))
        hidden_act = (activated * up_proj).astype(BF)
        act_ref[rows] = hidden_act
        send(rows, 1, act_ref, act_hbm)
        need("down")
        out_ref[rows] = (score * dot(hidden_act, down_ref[...])).astype(BF)
        send(rows, 2, out_ref, out_hbm)
        need("cots")
        cot = cots_ref[rows]
        act_raw = dot(cot, down_ref[...], ((1,), (1,)))
        score_grad = jnp.sum(hidden_act.astype(F32) * act_raw, axis=1, keepdims=True)
        logit_cot = score_grad * score * (1.0 - score)
        out_cot_ref[rows] = (score * cot.astype(F32)).astype(BF)
        send(rows, 3, out_cot_ref, out_cot_hbm)
        act_cot = score * act_raw
        gate_cot = (act_cot * factor).astype(BF)
        up_cot = (act_cot * activated).astype(BF)
        gate_cot_ref[rows] = gate_cot
        send(rows, 4, gate_cot_ref, gate_cot_hbm)
        up_cot_ref[rows] = up_cot
        send(rows, 5, up_cot_ref, up_cot_hbm)
        slot_cot = dot(gate_cot, gate_ref[...], ((1,), (1,))) + dot(up_cot, up_ref[...], ((1,), (1,)))
        upstream = slot_cot + logit_cot * router_ref[...]
        scaled = upstream * gain_ref[...]
        mean = jnp.mean(scaled * normed, axis=-1, keepdims=True)
        embed_cot = (inv_rms * (scaled - normed * mean)).astype(BF)
        embed_cot_ref[rows] = embed_cot
        router_sum += jnp.sum(hidden.astype(F32) * logit_cot, axis=0, keepdims=True)
        gain_sum += jnp.sum(upstream * normed, axis=0, keepdims=True)
        feature_cot = dot(embed_cot, embed_ref[...], ((1,), (1,)))
        preact_cot_ref[rows] = (feature_cot * slope).astype(BF)

    product_sum = dot(cells_ref[...], preact_cot_ref[...], ((0,), (0,)))
    need("place")
    taps = dot(place_ref[...], product_sum.astype(BF))
    col = lax.broadcasted_iota(jnp.int32, (TAPS, pixels), 1)
    wide = jnp.zeros((TAPS, pixels), F32)
    for cell in range(16):
        wide += jnp.where(col % 16 == cell, taps[cell * TAPS : cell * TAPS + TAPS], 0.0)
    chan = lax.broadcasted_iota(jnp.int32, (LANES, pixels), 0)
    group = lax.broadcasted_iota(jnp.int32, (LANES, pixels), 1)
    stem = dot(wide.astype(BF), (chan == group // 16).astype(BF), ((1,), (1,)))
    router = folded(router_sum)
    gain = folded(gain_sum)
    expert, core = place_at_ref[0], place_at_ref[1]

    def small(p):
        if p < 32:
            return jnp.where(expert == p, router, 0.0)
        if p == 32:
            return gain
        if p < 38:
            return stem[8 * (p - 33) : 8 * (p - 33) + 8]
        return jnp.zeros((8, LANES), F32)

    part = pixels // 2
    for target, side in ((other_ref, 1 - core), (own_ref, core)):
        columns = pl.ds(pl.multiple_of(side * part, LANES), part)
        embed_part = dot(patches_ref[:, columns], embed_cot_ref[...], ((0,), (0,)))
        for a in range(part // TALL):
            for b in range(across):
                p = a * across + b
                main = embed_part[a * TALL : a * TALL + TALL, b * LANES : b * LANES + LANES]
                rest = jnp.where(side == 0, small(p), 0.0)
                target[p] = jnp.concatenate([main, rest], axis=0).astype(target.dtype)
    for copy in leaving:
        copy.wait()


def layer(place_at, gain, router_row, moved, conv, embed_weight, w_gate, w_up, w_down):
    total = moved.shape[0]
    width = gain.shape[1]
    units = w_gate.shape[1]
    pixels = conv.shape[1]
    place = jnp.asarray(placement_rows(), BF)
    place = jnp.pad(place, ((0, 0), (0, moved.shape[1] - width - PIX)))
    outs = (width, width, units, units, units, width)
    return pl.pallas_call(
        layer_kernel,
        in_specs=[SMEM, VMEM, VMEM] + [HBM] * 7,
        out_specs=[HBM] * len(outs) + [VMEM] * 2,
        out_shape=[jax.ShapeDtypeStruct((total, size), BF) for size in outs]
        + [
            jax.ShapeDtypeStruct((64, TALL + 8, LANES), F32),
            jax.ShapeDtypeStruct((64, TALL + 8, LANES), BF),
        ],
        scratch_shapes=[
            pltpu.VMEM((total, moved.shape[1] - width), BF),
            pltpu.VMEM(conv.shape, BF),
            pltpu.VMEM(embed_weight.shape, BF),
            pltpu.VMEM(w_gate.shape, BF),
            pltpu.VMEM(w_up.shape, BF),
            pltpu.VMEM(w_down.shape, BF),
            pltpu.VMEM((total, width), BF),
            pltpu.VMEM(place.shape, BF),
        ]
        + [pltpu.VMEM((total, size), BF) for size in (*outs, pixels, width, pixels)]
        + [pltpu.SemaphoreType.DMA((8,)), pltpu.SemaphoreType.DMA((total // ROWS, len(outs)))],
        compiler_params=pltpu.CompilerParams(vmem_limit_bytes=52 << 20),
        cost_estimate=pl.CostEstimate(flops=18 << 30, bytes_accessed=30 << 20, transcendentals=0),
    )(place_at, gain, router_row, moved, conv, embed_weight, w_gate, w_up, w_down, place)


def finish_kernel(core_ref, mine_ref, theirs_ref, embed_ref, router_ref, gain_ref, stem_ref):
    first = core_ref[0] == 0
    count = mine_ref.shape[0]
    tall, lanes = 48, 128
    across = embed_ref.shape[1] // lanes

    def piece(p):
        near = mine_ref[p % count].astype(F32)
        far = theirs_ref[p % count].astype(F32)
        return jnp.where(first, near, far) if p < count else jnp.where(first, far, near)

    experts = router_ref.shape[1]
    rows = []
    for p in range(2 * count):
        value = piece(p)
        a, b = p // across, p % across
        embed_ref[a * tall : a * tall + tall, b * lanes : b * lanes + lanes] = value[:tall]
        if p < experts:
            rows.append(value[tall:])
        elif p == experts:
            gain_ref[...] = value[tall:]
        elif p < experts + 6:
            k = p - experts - 1
            stem_ref[8 * k : 8 * k + 8, :] = value[tall:]
    for k in range(across):
        block = jnp.concatenate([row[k : k + 1] for row in rows], axis=0)
        router_ref[k * lanes : k * lanes + lanes, :] = block.T


def finish(core, mine, theirs, pixels, width, experts):
    return pl.pallas_call(
        finish_kernel,
        in_specs=[
            pl.BlockSpec(memory_space=pltpu.SMEM),
            pl.BlockSpec(memory_space=pltpu.VMEM),
            pl.BlockSpec(memory_space=pltpu.VMEM),
        ],
        out_specs=[pl.BlockSpec(memory_space=pltpu.VMEM)] * 4,
        out_shape=[
            jax.ShapeDtypeStruct((pixels, width), F32),
            jax.ShapeDtypeStruct((width, experts), F32),
            jax.ShapeDtypeStruct((8, 128), F32),
            jax.ShapeDtypeStruct((TAPS, 128), F32),
        ],
        compiler_params=pltpu.CompilerParams(vmem_limit_bytes=32 << 20),
        cost_estimate=pl.CostEstimate(flops=1 << 20, bytes_accessed=6 << 20, transcendentals=0),
    )(core, mine, theirs)


def cell_mask(channels):
    cell = lax.broadcasted_iota(jnp.int32, (16, channels * 16), 0)
    col = lax.broadcasted_iota(jnp.int32, (16, channels * 16), 1)
    return cell == col % 16


def spread(channels):
    chan = lax.broadcasted_iota(jnp.int32, (channels, channels * 16), 0)
    col = lax.broadcasted_iota(jnp.int32, (channels, channels * 16), 1)
    return (chan == col // 16).astype(BF)


def stem_matrix(stem_weight):
    channels = stem_weight.shape[0]
    taps = stem_weight.reshape(channels, 36)
    wide = dot(taps, spread(channels), ((0,), (0,))).astype(BF)
    stack = jnp.where(cell_mask(channels)[:, None, :], wide[None], BF(0))
    return dot(jnp.asarray(placement(), BF), stack.reshape(16 * 36, channels * 16)).astype(BF)


def slots_of(route, experts, capacity):
    tokens = route.shape[0]
    hot = (route[:, None] == jnp.arange(experts, dtype=jnp.int32)[None, :]).astype(F32)
    row = lax.broadcasted_iota(jnp.int32, (tokens, tokens), 0)
    col = lax.broadcasted_iota(jnp.int32, (tokens, tokens), 1)
    before = dot((col < row).astype(BF), hot.astype(BF))
    return route * capacity + jnp.sum(before * hot, axis=1).astype(jnp.int32)


def swap(block):
    count = lax.axis_size("core")
    return lax.ppermute(block, "core", [(i, count - 1 - i) for i in range(count)])


def total_over_all(own, other, beside):
    chip = (own + swap(other).astype(F32)).astype(BF)
    parts = lax.all_to_all(chip, HALF, split_axis=0, concat_axis=0, tiled=True)
    parts, done = lax.optimization_barrier((parts, beside(chip)))
    total = jnp.sum(parts.astype(F32), axis=0).astype(BF)
    copies = jnp.broadcast_to(total[None], parts.shape)
    mine = lax.all_to_all(copies, HALF, split_axis=0, concat_axis=0, tiled=True)
    theirs = swap(mine)
    return mine, theirs, done


def to_owners(rows, members):
    copies = jnp.broadcast_to(rows[None], (members, *rows.shape))
    blocks = copies.reshape(lax.axis_size(ALL), -1, rows.shape[1])
    moved = lax.all_to_all(blocks, ALL, split_axis=0, concat_axis=0, tiled=True)
    return moved.reshape(-1, rows.shape[1])


def local(
    raw_tiles,
    stem_weight,
    embed_weight,
    norm_gain,
    router_weight,
    w_gate,
    w_up,
    w_down,
    routes,
    cotangent,
):
    tokens, width = cotangent.shape
    owners = lax.axis_size(DE)
    members = lax.axis_size("tp")
    devices = owners * members
    experts = owners
    capacity = 2 * tokens // experts
    slots = experts * capacity
    w_gate, w_up, w_down = w_gate[0], w_up[0], w_down[0]

    slot_of = slots_of(routes[:, 0], experts, capacity)
    selector = (slot_of[None, :] == jnp.arange(slots, dtype=jnp.int32)[:, None]).astype(BF)
    windows = window_rows(halo_rows(raw_tiles), tokens)
    windows = jnp.pad(windows, ((0, 0), (0, -PIX % 128)))
    sent = dot(selector, jnp.concatenate([cotangent, windows], axis=1)).astype(BF)
    moved = to_owners(lax.optimization_barrier(sent), members)

    conv = jnp.pad(stem_matrix(stem_weight), ((0, -PIX % 128), (0, 0)))
    expert = lax.axis_index(DE)
    router_row = lax.dynamic_slice_in_dim(router_weight, expert, 1, axis=1).reshape(1, width)
    router_row = router_row.astype(F32)
    gain = norm_gain.reshape(1, width)
    core = lax.axis_index("core").reshape(1)
    out_part, hidden, hidden_act, gate_cot, up_cot, out_cot, own, other = layer(
        jnp.concatenate([expert.reshape(1), core]),
        gain, router_row, moved, conv, embed_weight, w_gate, w_up, w_down,
    )
    out_share = lax.psum_scatter(out_part, "tp", scatter_dimension=0, tiled=True)
    mixed = out_share.reshape(experts, capacity, width)
    returned = lax.all_to_all(mixed, DE, split_axis=0, concat_axis=0, tiled=True)
    expert_mix = dot(selector, returned.reshape(slots, width), ((0,), (0,))).astype(BF)

    def weight_grads(ready):
        rows, gates, ups, acts, outs, _ = lax.optimization_barrier(
            (hidden, gate_cot, up_cot, hidden_act, out_cot, ready)
        )
        return (
            dot(rows, gates, ((0,), (0,))),
            dot(rows, ups, ((0,), (0,))),
            dot(acts, outs, ((0,), (0,))),
        )

    mine, theirs, grads = total_over_all(own, other, weight_grads)
    embed_total, router_total, gain_total, stem_total = finish(
        core, mine, theirs, embed_weight.shape[0], width, experts
    )
    stem_total = stem_total[:36, : stem_weight.shape[0]].T
    return (
        expert_mix,
        grads[0][None],
        grads[1][None],
        grads[2][None],
        router_total,
        gain_total.reshape(width),
        embed_total,
        stem_total.reshape(stem_weight.shape),
    )


def solution(mesh):
    owners, members = mesh.devices.shape
    fine = jax.sharding.Mesh(mesh.devices.reshape(owners // 2, 2, members), ("xz", "core", "tp"))
    return jax.shard_map(
        local,
        mesh=fine,
        in_specs=(
            P(None, DE_TP, None),
            P(),
            P(),
            P(),
            P(),
            P(DE, None, "tp"),
            P(DE, None, "tp"),
            P(DE, "tp", None),
            P(DE_TP, None),
            P(DE_TP, None),
        ),
        out_specs=(
            P(DE_TP, None),
            P(DE, None, "tp"),
            P(DE, None, "tp"),
            P(DE, "tp", None),
            P(),
            P(),
            P(),
            P(),
        ),
        check_vma=False,
    )
```

time: 221 us -> 180 us (0.81)
  matrix products: 68.8 us -> 19.7 us
  Pallas kernels: 0 us -> 30.6 us
  local copies, waits for them, and re-layouts: 28.2 us -> 4.75 us
  waiting for transfers between devices: 26.7 us -> 43.7 us
  other arithmetic: 15.3 us -> 4.82 us
  starting transfers between devices: 38.7 us -> 33.5 us
    dot_general x20 -> x8, matrix products: 68.3 us -> 19.3 us  [dot(): return lax.dot_general(a, b, (dims, ((), ())), preferred_element_type=F32)]
    pallas_call x0 -> x2, Pallas kernels: none -> 30.6 us  [the longest x1 28.5 us: layer(): pl.pallas_call(layer_kernel, in_specs=[SMEM, VMEM, VMEM] + [HBM] * 7, out...]
    unnamed x50 -> x21, local copies, waits for them, and re-layouts: 14.5 us -> 1.79 us
    all_to_all x3 -> x2, waiting for transfers between devices: 23.1 us -> 33.4 us  [the longest x1 33.3 us: to_owners(): moved = lax.all_to_all(blocks, ALL, split_axis=0, concat_axis=0, tiled=True)]
    reshape x4 -> x0, local copies, waits for them, and re-layouts: 7.28 us -> none  [the longest x1 3.96 us: local(): cots = lax.all_gather(moved, 'tp', axis=0, tiled=True).reshape(total, width)]
    all_to_all x1, waiting for transfers between devices: 1.6 us -> 8.02 us  [local(): lax.all_to_all(mixed, DE, split_axis=0, concat_axis=0, tiled=True)]
    all_to_all x3 -> x2, starting transfers between devices: 21.9 us -> 17.6 us  [the longest x1 12.7 us: to_owners(): moved = lax.all_to_all(blocks, ALL, split_axis=0, concat_axis=0, tiled=True)]
    reshape x3 -> x0, other arithmetic: 2.99 us -> none  [the longest x1 2.03 us: local(): (out_share.astype(F32) * score_share).astype(BF)]
  transfers between devices with their start and end apart: 10 -> 8, of which waited for: 5 -> 4; matrix products, arithmetic and copies ran while one was open for 31% -> 13% of each run, Pallas kernels for 0% -> 1%
where the time goes in v3:
time: 180 us; the launch traced here: 176 us
  waiting for transfers between devices  43.7 us (24%)
  starting transfers between devices  33.5 us (19%)
  Pallas kernels  30.6 us (17%)
  blocking collectives  24.6 us (14%)
  matrix products  19.7 us (11%)
  between operations  14.7 us (8%)
  other arithmetic  4.82 us (3%)
  local copies, waits for them, and re-layouts  4.75 us (3%)
    all_to_all x1, waiting for transfers between devices, to_owners(): moved = lax.all_to_all(blocks, ALL, split_axis=0, concat_axis=0, tiled=True)  33.3 us
    pallas_call x1, Pallas kernels, layer(): pl.pallas_call(layer_kernel, in_specs=[SMEM, VMEM, VMEM] + [HBM] * 7, out...  28.5 us
    all_to_all x1, blocking collectives, total_over_all(): mine = lax.all_to_all(copies, HALF, split_axis=0, concat_axis=0, tiled=True)  24.6 us
    dot_general x8, matrix products, dot(): return lax.dot_general(a, b, (dims, ((), ())), preferred_element_type=F32)  19.3 us
    all_to_all x1, starting transfers between devices, to_owners(): moved = lax.all_to_all(blocks, ALL, split_axis=0, concat_axis=0, tiled=True)  12.7 us
    all_to_all x1, waiting for transfers between devices, local(): lax.all_to_all(mixed, DE, split_axis=0, concat_axis=0, tiled=True)  8.02 us
    all_to_all x1, starting transfers between devices, total_over_all(): parts = lax.all_to_all(chip, HALF, split_axis=0, concat_axis=0, tiled=True)  4.9 us
    ppermute x2, starting transfers between devices, swap(): lax.ppermute(block, 'core', [(i, count - 1 - i) for i in range(count)])  4.23 us
  transfers between devices with their start and end apart: 8, of which 4 were waited for; matrix products, arithmetic and copies ran while one was open for 13% of the time, Pallas kernels for 1%

profile of v3, /device:TPU:1, one launch (start us, length us, event | category | flops | bytes accessed | tf_op | source)
XLA Modules:
  0.0 176.4 jit_solution(8515475971361036140)
XLA Ops:
  7.2 0.8 fusion.31
  8.0 4.0 %collective-permute-start = (bf16[4,1,512]{2,1,0:T(2,128)(2,1)S(1)}, bf16[4,1,512]{2,1,0:T(2,128)(2,1)S(1)}, u32[]{:S(2)}, u32[]{:S(2)}) collective-permute-start(bf16[4,1,512]{2,1,0:T(2,128)(2,1)S(1)} %get-tuple-element.66), channel_id=1, source_target_pairs={{0,1},{1,2},{2,3},{3,4},{4,5},{5,6},{6,7},{7,8},{8,9},{9,10},{10,1... | collective-permute-start | bytes 12296 | tf_op jit(solution)/shard_map/ppermute | solution.py:30
  12.0 3.9 %collective-permute-start.1 = (bf16[4,1,512]{2,1,0:T(2,128)(2,1)S(1)}, bf16[4,1,512]{2,1,0:T(2,128)(2,1)S(1)}, u32[]{:S(2)}, u32[]{:S(2)}) collective-permute-start(bf16[4,1,512]{2,1,0:T(2,128)(2,1)S(1)} %get-tuple-element.67), channel_id=1, source_target_pairs={{1,0},{2,1},{3,2},{4,3},{5,4},{6,5},{7,6},{8,7},{9,8},{10,9},{11,1... | collective-permute-start | bytes 12296 | tf_op jit(solution)/shard_map/ppermute | solution.py:31
  15.9 0.9 fusion.4
  16.8 0.7 convert_add_fusion
  17.5 0.8 pad_maximum_fusion
  18.3 0.5 fusion.3
  18.9 1.3 convolution_convert_fusion
  20.2 1.7 broadcast_in_dim.46
  21.8 12.7 %all-to-all-start = ((bf16[128,8,1280]{2,1,0:T(8,128)(2,1)}), bf16[128,8,1280]{2,1,0:T(8,128)(2,1)}, u32[]{:S(2)}, u32[]{:S(2)}) async-start(bf16[128,8,1280]{2,1,0:T(8,128)(2,1)} %bitcast.7), calls=%async_computation | async-start | bytes 5242880 | tf_op jit(solution)/shard_map/all_to_all | solution.py:340
  35.0 0.2 select_n.31
  35.2 0.3 copy-done.3
  35.5 0.3 fusion.1
  36.0 0.7 bitcast_convert_fusion.router_ref
  36.7 33.3 %all-to-all-done = bf16[128,8,1280]{2,1,0:T(8,128)(2,1)} async-done(((bf16[128,8,1280]{2,1,0:T(8,128)(2,1)}), bf16[128,8,1280]{2,1,0:T(8,128)(2,1)}, u32[]{:S(2)}, u32[]{:S(2)}) %all-to-all-start) | async-done | bytes 2621472 | tf_op jit(solution)/shard_map/all_to_all | solution.py:340
  70.0 28.5 %shard_map.179 = (bf16[1024,1024]{1,0:T(8,128)(2,1)}, bf16[1024,1024]{1,0:T(8,128)(2,1)}, bf16[1024,1024]{1,0:T(8,128)(2,1)}, bf16[1024,1024]{1,0:T(8,128)(2,1)}...) custom-call(s32[2]{0:T(128)S(1)} %pad_add_fusion.place_at_ref, ...), custom_call_target="tpu_custom_call" | custom-call | flops 19327352832 | bytes 31457280 | tf_op jit(solution)/shard_map/pallas_call | solution.py:217
  98.6 1.4 collective-permute-start.2
  100.0 2.2 %collective-permute-done.2 = bf16[64,56,128]{2,1,0:T(8,128)(2,1)} collective-permute-done((bf16[64,56,128]{2,1,0:T(8,128)(2,1)S(1)}, bf16[64,56,128]{2,1,0:T(8,128)(2,1)}, u32[]{:S(2)}, u32[]{:S(2)}) %collective-permute-start.2) | collective-permute-done | bytes 917536 | tf_op jit(solution)/shard_map/ppermute | solution.py:323
  102.2 2.3 %add_convert_fusion = bf16[64,56,128]{2,1,0:T(8,128)(2,1)} fusion(f32[64,56,128]{2,1,0:T(8,128)S(1)} %copy-done.2, bf16[64,56,128]{2,1,0:T(8,128)(2,1)} %collective-permute-done.2), kind=kLoop, calls=%fused_computation.1 | loop fusion | flops 1376256 | bytes 3670016 | tf_op jit(solution)/shard_map/convert_element_type | solution.py:327
  104.5 4.9 %all-to-all-start.2 = ((bf16[64,56,128]{2,1,0:T(8,128)(2,1)}), bf16[64,56,128]{2,1,0:T(8,128)(2,1)S(1)}, u32[]{:S(2)}, u32[]{:S(2)}) async-start(bf16[64,56,128]{2,1,0:T(8,128)(2,1)} %add_convert_fusion), calls=%async_computation.3 | async-start | bytes 1835008 | tf_op jit(solution)/shard_map/all_to_all | solution.py:328
  109.5 6.8 %fusion.32 = f32[1024,1024]{1,0:T(8,128)} fusion(bf16[1024,1024]{1,0:T(8,128)(2,1)} %get-tuple-element.37, bf16[1024,1024]{1,0:T(8,128)(2,1)} %get-tuple-element.38), kind=kOutput, calls=%fused_computation.56 | convolution fusion | flops 2147483648 | bytes 8388608 | tf_op jit(solution)/shard_map/dot_general | solution.py:23
  116.3 4.4 %fusion.33 = f32[1024,1024]{1,0:T(8,128)} fusion(bf16[1024,1024]{1,0:T(8,128)(2,1)S(1)} %copy-done.7, bf16[1024,1024]{1,0:T(8,128)(2,1)S(1)} %copy-done.8), kind=kOutput, calls=%fused_computation.57 | convolution fusion | flops 2147483648 | bytes 8388608 | tf_op jit(solution)/shard_map/dot_general | solution.py:23
  120.7 4.4 %fusion.34 = f32[1024,1024]{1,0:T(8,128)} fusion(bf16[1024,1024]{1,0:T(8,128)(2,1)S(1)} %copy-done.5, bf16[1024,1024]{1,0:T(8,128)(2,1)S(1)} %copy-done.6), kind=kOutput, calls=%fused_computation.58 | convolution fusion | flops 2147483648 | bytes 8388608 | tf_op jit(solution)/shard_map/dot_general | solution.py:23
  125.2 0.2 reduce_sum.22
  125.5 24.6 %all_to_all.20.mine_ref = bf16[64,56,128]{2,1,0:T(8,128)(2,1)S(1)} all-to-all(bf16[64,56,128]{2,1,0:T(8,128)(2,1)S(1)} %broadcast_in_dim.53), channel_id=1, replica_groups=mesh['xz'=16,'core'=2,'tp'=4] {'xz','tp'}, dimensions={0} | all-to-all | bytes 1835008 | tf_op jit(solution)/shard_map/all_to_all | solution.py:332
  150.1 2.8 %collective-permute-start.3 = (bf16[64,56,128]{2,1,0:T(8,128)(2,1)S(1)}, bf16[64,56,128]{2,1,0:T(8,128)(2,1)S(1)}, u32[]{:S(2)}, u32[]{:S(2)}) collective-permute-start(bf16[64,56,128]{2,1,0:T(8,128)(2,1)S(1)} %all_to_all.20.mine_ref), channel_id=1, source_target_pairs={{0,4},{4,0},{1,5},{5,1},{2,6},{6,2},{3,7},{7,3},{8,12},{12,8},{9,1... | collective-permute-start | bytes 2752520 | tf_op jit(solution)/shard_map/ppermute | solution.py:323
  152.9 3.7 %all-to-all-start.1 = ((bf16[32,8,1024]{2,1,0:T(8,128)(2,1)}), bf16[32,8,1024]{2,1,0:T(8,128)(2,1)S(1)}, u32[]{:S(2)}, u32[]{:S(2)}) async-start(bf16[32,8,1024]{2,1,0:T(8,128)(2,1)} %bitcast.45), calls=%async_computation.2 | async-start | bytes 1048576 | tf_op jit(solution)/shard_map/all_to_all | solution.py:384
  156.6 2.1 %shard_map.180 = (f32[768,1024]{1,0:T(8,128)}, f32[1024,32]{1,0:T(8,128)S(1)}, f32[8,128]{1,0:T(8,128)}, f32[40,128]{1,0:T(8,128)S(1)}) custom-call(s32[1]{0:T(128)} %bitcast.2.core_ref, bf16[64,56,128]{2,1,0:T(8,128)(2,1)S(1)} %all_to_all.20.mine_ref, bf16[64,56,128]{2,1,0:T(8,128)(2,1)S(1)} %collective-permute-done.3.theirs_ref), custom_call_target="tpu_custom_call" | custom-call | flops 1048576 | bytes 6291456 | tf_op jit(solution)/shard_map/pallas_call | solution.py:273
  158.7 0.8 copy.25
  159.5 0.6 copy.26
  160.2 8.0 %all-to-all-done.1 = bf16[32,8,1024]{2,1,0:T(8,128)(2,1)S(1)} async-done(((bf16[32,8,1024]{2,1,0:T(8,128)(2,1)}), bf16[32,8,1024]{2,1,0:T(8,128)(2,1)S(1)}, u32[]{:S(2)}, u32[]{:S(2)}) %all-to-all-start.1) | async-done | bytes 524320 | tf_op jit(solution)/shard_map/all_to_all | solution.py:384
  168.2 1.0 convolution_convert_fusion.1
  (41 shorter events, 0.9 us)
Async XLA Ops:
  8.0 9.5 %collective-permute-start = (bf16[4,1,512]{2,1,0:T(2,128)(2,1)S(1)}, bf16[4,1,512]{2,1,0:T(2,128)(2,1)S(1)}, u32[]{:S(2)}, u32[]{:S(2)}) collective-permute-start(bf16[4,1,512]{2,1,0:T(2,128)(2,1)S(1)} %get-tuple-element.66), channel_id=1, source_target_pairs={{0,1},{1,2},{2,3},{3,4},{4,5},{5,6},{6,7},{7,8},{8,9},{9,10},{10,1... | collective-permute-start | bytes 12296 | tf_op jit(solution)/shard_map/ppermute | solution.py:30
  12.0 5.5 %collective-permute-start.1 = (bf16[4,1,512]{2,1,0:T(2,128)(2,1)S(1)}, bf16[4,1,512]{2,1,0:T(2,128)(2,1)S(1)}, u32[]{:S(2)}, u32[]{:S(2)}) collective-permute-start(bf16[4,1,512]{2,1,0:T(2,128)(2,1)S(1)} %get-tuple-element.67), channel_id=1, source_target_pairs={{1,0},{2,1},{3,2},{4,3},{5,4},{6,5},{7,6},{8,7},{9,8},{10,9},{11,1... | collective-permute-start | bytes 12296 | tf_op jit(solution)/shard_map/ppermute | solution.py:31
  21.8 12.8 %copy-start.4 = (bf16[48,4,3,3]{0,1,3,2:T(4,128)(2,1)S(1)}, bf16[48,4,3,3]{0,1,3,2:T(4,128)(2,1)}, u32[]{:S(2)}) copy-start(bf16[48,4,3,3]{0,1,3,2:T(4,128)(2,1)} %param.13) | copy-start | bytes 10372
  21.8 48.2 %all-to-all-start = ((bf16[128,8,1280]{2,1,0:T(8,128)(2,1)}), bf16[128,8,1280]{2,1,0:T(8,128)(2,1)}, u32[]{:S(2)}, u32[]{:S(2)}) async-start(bf16[128,8,1280]{2,1,0:T(8,128)(2,1)} %bitcast.7), calls=%async_computation | async-start | bytes 5242880 | tf_op jit(solution)/shard_map/all_to_all | solution.py:340
  34.6 0.9 copy-start.3
  34.6 118.3 %reduce-scatter.2.cloned.1.call-start = ((), (), s32[]{:S(2)}) async-start(), calls=%async_computation.5 | async-start | bytes 2621440 | tf_op jit(solution)/shard_map/reduce_scatter | solution.py:382
  35.0 35.0 %copy-start = (f32[1024]{0:T(1024)S(1)}, f32[1024]{0:T(1024)}, u32[]{:S(2)}) copy-start(f32[1024]{0:T(1024)} %param.15) | copy-start | bytes 12292
  35.0 35.0 %copy-start.1 = (bf16[640,256]{1,0:T(8,128)(2,1)S(1)}, bf16[640,256]{1,0:T(8,128)(2,1)}, u32[]{:S(2)}) copy-start(bf16[640,256]{1,0:T(8,128)(2,1)} %constant.78.place_hbm) | copy-start | bytes 983044
  98.5 3.7 %copy-start.2 = (f32[64,56,128]{2,1,0:T(8,128)S(1)}, f32[64,56,128]{2,1,0:T(8,128)}, u32[]{:S(2)}) copy-start(f32[64,56,128]{2,1,0:T(8,128)} %get-tuple-element.30) | copy-start | bytes 5505028
  98.6 3.7 %collective-permute-start.2 = (bf16[64,56,128]{2,1,0:T(8,128)(2,1)S(1)}, bf16[64,56,128]{2,1,0:T(8,128)(2,1)}, u32[]{:S(2)}, u32[]{:S(2)}) collective-permute-start(bf16[64,56,128]{2,1,0:T(8,128)(2,1)S(1)} %get-tuple-element.31), channel_id=1, source_target_pairs={{0,4},{4,0},{1,5},{5,1},{2,6},{6,2},{3,7},{7,3},{8,12},{12,8},{9,1... | collective-permute-start | bytes 2752520 | tf_op jit(solution)/shard_map/ppermute | solution.py:323
  104.5 20.7 %all-to-all-start.2 = ((bf16[64,56,128]{2,1,0:T(8,128)(2,1)}), bf16[64,56,128]{2,1,0:T(8,128)(2,1)S(1)}, u32[]{:S(2)}, u32[]{:S(2)}) async-start(bf16[64,56,128]{2,1,0:T(8,128)(2,1)} %add_convert_fusion), calls=%async_computation.3 | async-start | bytes 1835008 | tf_op jit(solution)/shard_map/all_to_all | solution.py:328
  109.4 6.9 %copy-start.7 = (bf16[1024,1024]{1,0:T(8,128)(2,1)S(1)}, bf16[1024,1024]{1,0:T(8,128)(2,1)}, u32[]{:S(2)}) copy-start(bf16[1024,1024]{1,0:T(8,128)(2,1)} %get-tuple-element.37) | copy-start | bytes 6291460
  109.5 6.8 %copy-start.8 = (bf16[1024,1024]{1,0:T(8,128)(2,1)S(1)}, bf16[1024,1024]{1,0:T(8,128)(2,1)}, u32[]{:S(2)}) copy-start(bf16[1024,1024]{1,0:T(8,128)(2,1)} %get-tuple-element.39) | copy-start | bytes 6291460
  116.3 4.4 %copy-start.5 = (bf16[1024,1024]{1,0:T(8,128)(2,1)S(1)}, bf16[1024,1024]{1,0:T(8,128)(2,1)}, u32[]{:S(2)}) copy-start(bf16[1024,1024]{1,0:T(8,128)(2,1)} %get-tuple-element.40) | copy-start | bytes 6291460
  116.3 4.4 %copy-start.6 = (bf16[1024,1024]{1,0:T(8,128)(2,1)S(1)}, bf16[1024,1024]{1,0:T(8,128)(2,1)}, u32[]{:S(2)}) copy-start(bf16[1024,1024]{1,0:T(8,128)(2,1)} %get-tuple-element.41) | copy-start | bytes 6291460
  150.1 6.5 %collective-permute-start.3 = (bf16[64,56,128]{2,1,0:T(8,128)(2,1)S(1)}, bf16[64,56,128]{2,1,0:T(8,128)(2,1)S(1)}, u32[]{:S(2)}, u32[]{:S(2)}) collective-permute-start(bf16[64,56,128]{2,1,0:T(8,128)(2,1)S(1)} %all_to_all.20.mine_ref), channel_id=1, source_target_pairs={{0,4},{4,0},{1,5},{5,1},{2,6},{6,2},{3,7},{7,3},{8,12},{12,8},{9,1... | collective-permute-start | bytes 2752520 | tf_op jit(solution)/shard_map/ppermute | solution.py:323
  152.9 15.3 %all-to-all-start.1 = ((bf16[32,8,1024]{2,1,0:T(8,128)(2,1)}), bf16[32,8,1024]{2,1,0:T(8,128)(2,1)S(1)}, u32[]{:S(2)}, u32[]{:S(2)}) async-start(bf16[32,8,1024]{2,1,0:T(8,128)(2,1)} %bitcast.45), calls=%async_computation.2 | async-start | bytes 1048576 | tf_op jit(solution)/shard_map/all_to_all | solution.py:384
Sparse Core Ops, SparseCore 0:
  100.1 34.3 reduce-scatter.1
